TPU v7x, 1024 devices: a whole 4x4x32 slice. The times are simulated.
1024 devices in a mesh: rows: 256 (over x, z, core), cols: 4 (over y).
Axes of the slice: x: 4, y: 4, z: 32, core: 2. Of those that a mesh axis runs over, the one named last changes fastest.
Arguments:
- rhs: float32 [2048, 8192], P('rows', 'cols'), may hold values from -6 to 6
- cond_row: float32 [2048, 8192], P('rows', 'cols'), may hold values from 0.3 to 3
- cond_col: float32 [2048, 8192], P('rows', 'cols'), may hold values from 0.3 to 3
- leak: float32 [2048, 8192], P('rows', 'cols'), may hold values from 0.01 to 0.2
- agg_members: int32 [256, 4, 192, 128], P('rows', 'cols'), may hold values from -1 to 16383, as said below
- coarse_inverse: float32 [4, 1024, 1024], P('cols', 'rows'), as said below
Outputs:
- potential: float32 [2048, 8192], P('rows', 'cols')
Inputs may be any that keep to these rules, and one draw needn't show every extreme that they name: `agg_members`: every node of a device's block is listed exactly once; aggregates are runs of consecutive node numbers in order, of 16 to 128 members, three consecutive aggregates covering 256 nodes, one of each three exactly 128; padding follows the members. Each coarse_inverse[c] is symmetric and positive definite.
All inputs are finite; a program needn't handle non-finite values.
Results may differ from a plain program's by a relative error of at most 0.0003.
Values sent between devices are 32-bit elements; how exact they have to be, the bound alone decides.
No kernel may reach another device: no remote copies, remote signals or barrier semaphores. Data moves between devices by JAX's collectives and lax.ppermute only.
A program may use at most 32 MiB of HBM per device.

v0:
```python
import jax
import jax.numpy as jnp
from jax import lax
from jax.sharding import PartitionSpec as P

theta_cheb = 1.05
delta_cheb = 0.95
omega_sa = 2.0 / 3.0


def with_halo(shard, sides, width):
    for axis, dim in sides:
        size, length = (lax.axis_size(axis), shard.shape[dim])
        up = [(i, (i + 1) % size) for i in range(size - 1)]
        down = [(j, i) for i, j in up]
        last = lax.slice_in_dim(shard, length - width, length, axis=dim)
        leading = lax.slice_in_dim(shard, 0, width, axis=dim)
        before = lax.ppermute(last, axis, up)
        after = lax.ppermute(leading, axis, down)
        shard = jnp.concatenate([before, shard, after], axis=dim)
    return shard


def passed_along(block, axis, distance):
    devices = range(lax.axis_size(axis))
    route = [(i - distance, i) for i in devices if i - distance in devices]
    return lax.ppermute(block, axis, route)


def stencil(padded, field, cond_row, cond_col, west, north, diag):
    out = diag * field - cond_row * padded[1:-1, 2:] - west * padded[1:-1, :-2]
    return out - cond_col * padded[2:, 1:-1] - north * padded[:-2, 1:-1]


def operate(field, cond_row, cond_col, west, north, diag):
    padded = with_halo(field, (("rows", 0), ("cols", 1)), 1)
    return stencil(padded, field, cond_row, cond_col, west, north, diag)


def chebyshev(start, right, apply_op, diag):
    if start is None:
        resid = right
    else:
        resid = right - apply_op(start)
    step = resid / (theta_cheb * diag)
    value = step if start is None else start + step
    rho = delta_cheb / theta_cheb
    for turn in range(2):
        rho_new = 1.0 / (2.0 * theta_cheb / delta_cheb - rho)
        resid = resid - apply_op(step)
        step = rho_new * rho * step + 2.0 * rho_new / delta_cheb * (resid / diag)
        value = value + step
        rho = rho_new
    return value


def local(rhs, cond_row, cond_col, leak, agg_members, coarse_inverse):
    left_links = passed_along(cond_row[:, -1:], "cols", 1)
    upper_links = passed_along(cond_col[-1:, :], "rows", 1)
    west = jnp.concatenate([left_links, cond_row[:, :-1]], axis=1)
    north = jnp.concatenate([upper_links, cond_col[:-1, :]], axis=0)
    diag = leak + cond_row + cond_col + west + north

    def apply_op(field):
        return operate(field, cond_row, cond_col, west, north, diag)

    pre = chebyshev(None, rhs, apply_op, diag)
    resid = rhs - apply_op(pre)
    smoothed = resid - omega_sa * apply_op(resid / diag)
    members = agg_members[0, 0]
    naggs = members.shape[0]
    triples = naggs // 3
    valid = members >= 0
    count_int = jnp.sum(valid, axis=-1)
    counts = count_int.astype(jnp.float32)
    starts = members[:, 0].reshape(triples, 3)
    ends = starts + count_int.reshape(triples, 3)
    position = (
        jnp.arange(triples, dtype=jnp.int32)[:, None] * 256
        + jnp.arange(256, dtype=jnp.int32)[None, :]
    )
    belong = (position[:, None, :] >= starts[:, :, None]) & (
        position[:, None, :] < ends[:, :, None]
    )
    tiles = smoothed.reshape(triples, 256)
    sums = jnp.sum(jnp.where(belong, tiles[:, None, :], jnp.float32(0.0)), axis=-1).reshape(naggs)
    fine_coarse = sums / jnp.sqrt(counts)
    ncoarse = coarse_inverse.shape[1]
    group = naggs // ncoarse
    coarse_rhs = fine_coarse.reshape(ncoarse, group).sum(-1) / jnp.sqrt(jnp.float32(group))
    own_rows = coarse_inverse[0]
    whole_rhs = lax.all_gather(coarse_rhs, "rows", axis=0, tiled=True)
    coarse_corr = jnp.dot(own_rows, whole_rhs, precision=lax.Precision.HIGHEST)
    agg_vals = jnp.repeat(coarse_corr / jnp.sqrt(jnp.float32(group)), group)
    scaled = (agg_vals / jnp.sqrt(counts)).reshape(triples, 3)
    lifted = jnp.sum(jnp.where(belong, scaled[:, :, None], jnp.float32(0.0)), axis=1).reshape(
        rhs.shape
    )
    corrected = pre + lifted - omega_sa * apply_op(lifted) / diag
    return chebyshev(corrected, rhs, apply_op, diag)


def solution(mesh):
    in_specs = (
        P("rows", "cols"),
        P("rows", "cols"),
        P("rows", "cols"),
        P("rows", "cols"),
        P("rows", "cols", None, None),
        P("cols", "rows", None),
    )
    out_specs = P("rows", "cols")
    return jax.shard_map(local, mesh=mesh, in_specs=in_specs, out_specs=out_specs, check_vma=False)
```

profile of v0, /device:TPU:1, one launch (start us, length us, event | category | flops | bytes accessed | tf_op | source)
XLA Modules:
  0.0 636.7 jit_solution(3816337508585085532)
XLA Ops:
  0.9 4.9 collective-permute-start.1
  6.6 3.2 collective-permute-start
  10.5 6.5 %collective-permute-done.1 = f32[1,2048]{1,0:T(1,128)S(1)} collective-permute-done((f32[1,2048]{1,0:T(1,128)S(1)}, f32[1,2048]{1,0:T(1,128)S(1)}, u32[]{:S(2)}, u32[]{:S(2)}) %collective-permute-start.1) | collective-permute-done | bytes 8224 | tf_op jit(solution)/shard_map/ppermute | solution.py:27
  20.2 4.0 collective-permute-start.3
  26.5 4.4 collective-permute-start.5
  36.6 3.0 collective-permute-done.7
  40.9 4.5 collective-permute-start.9
  46.5 2.8 collective-permute-start.10
  51.4 2.9 collective-permute-done.11
  55.7 4.5 collective-permute-start.13
  61.2 2.8 collective-permute-start.14
  70.3 4.5 collective-permute-start.17
  76.5 501.0 %all-reduce = f32[1024]{0:T(1024)S(1)} all-reduce(f32[1024]{0:T(1024)S(1)} %multiply_dynamic-update-slice_fusion), channel_id=1, replica_groups=mesh['rows'=256,'cols'=4] {'rows'}, use_global_device_ids=true, to_apply=%add | all-reduce | flops 1024 | bytes 8192
  579.9 4.4 collective-permute-start.19
  586.5 4.3 collective-permute-start.21
  591.9 2.8 collective-permute-start.22
  596.7 3.0 collective-permute-done.23
  601.1 4.5 collective-permute-start.25
  606.6 2.8 collective-permute-start.26
  611.3 3.0 collective-permute-done.27
  615.7 4.5 collective-permute-start.29
  621.3 2.8 collective-permute-start.30
  626.1 3.0 collective-permute-done.31
  630.5 4.5 collective-permute-start.33
  (110 shorter events, 46.7 us)
Async XLA Ops:
  0.9 16.1 %collective-permute-start.1 = (f32[1,2048]{1,0:T(1,128)S(1)}, f32[1,2048]{1,0:T(1,128)S(1)}, u32[]{:S(2)}, u32[]{:S(2)}) collective-permute-start(f32[1,2048]{1,0:T(1,128)S(1)} %slice.247), channel_id=1, source_target_pairs={{0,4},{4,8},{8,12},{12,16},{16,20},{20,24},{24,28},{28,32},{32,36}... | collective-permute-start | bytes 24584 | tf_op jit(solution)/shard_map/ppermute | solution.py:27
  18.1 6.1 collective-permute-start.2
  20.2 5.0 collective-permute-start.3
  25.2 5.7 collective-permute-start.4
  26.5 5.2 collective-permute-start.5
  34.6 5.0 collective-permute-start.7
  39.6 5.8 collective-permute-start.8
  40.9 5.3 collective-permute-start.9
  49.3 5.0 collective-permute-start.11
  54.4 5.8 collective-permute-start.12
  55.7 5.3 collective-permute-start.13
  61.2 7.3 %collective-permute-start.14 = (f32[1,2048]{1,0:T(1,128)S(1)}, f32[1,2048]{1,0:T(1,128)S(1)}, u32[]{:S(2)}, u32[]{:S(2)}) collective-permute-start(f32[1,2048]{1,0:T(1,128)S(1)} %get-tuple-element.30), channel_id=1, source_target_pairs={{0,4},{4,8},{8,12},{12,16},{16,20},{20,24},{24,28},{28,32},{32,36}... | collective-permute-start | bytes 24584 | tf_op jit(solution)/shard_map/ppermute | solution.py:18
  69.0 5.8 collective-permute-start.16
  70.3 5.3 collective-permute-start.17
  578.0 6.4 collective-permute-start.18
  579.9 5.2 collective-permute-start.19
  585.2 5.6 collective-permute-start.20
  586.5 5.1 collective-permute-start.21
  599.8 5.8 collective-permute-start.24
  601.1 5.3 collective-permute-start.25
  614.4 5.8 collective-permute-start.28
  615.7 5.3 collective-permute-start.29
  629.2 5.8 collective-permute-start.32
  630.5 5.3 collective-permute-start.33
  (16 other events, 686.7 us)
where the time goes:
time: 638 us; the launch traced here: 637 us
  blocking collectives  501 us (79%)
  starting transfers between devices  94.8 us (15%)
  waiting for transfers between devices  30.5 us (5%)
    unnamed x1, blocking collectives  501 us
    ppermute x16, starting transfers between devices, with_halo(): before = lax.ppermute(last, axis, up)  56.6 us
    ppermute x16, starting transfers between devices, with_halo(): after = lax.ppermute(leading, axis, down)  30.2 us
    ppermute x16, waiting for transfers between devices, with_halo(): after = lax.ppermute(leading, axis, down)  17.2 us
  transfers between devices with their start and end apart: 34, of which 18 were waited for; matrix products, arithmetic and copies ran while one was open for 0% of the time, Pallas kernels for 0%

commit v1 on v0

v1 whole, which is shorter than its diff:
```python
import functools

import jax
import jax.numpy as jnp
from jax import lax
from jax.experimental import pallas as pl
from jax.experimental.pallas import tpu as pltpu
from jax.sharding import Mesh
from jax.sharding import PartitionSpec as P

THETA = 1.05
DELTA = 0.95
OMEGA = 2.0 / 3.0
RHO0 = DELTA / THETA
RHO1 = 1.0 / (2.0 * THETA / DELTA - RHO0)
RHO2 = 1.0 / (2.0 * THETA / DELTA - RHO1)
LANES = 128
REACH = 5
WROWS = 24
MSG = 24
ROWAX = ("x", "z", "core")
VMEM_LIMIT = 48 * 1024 * 1024


def vmem():
    return pl.BlockSpec(memory_space=pltpu.VMEM)


def call(kernel, outs, nin, name):
    return pl.pallas_call(
        kernel,
        out_shape=outs,
        in_specs=[vmem()] * nin,
        out_specs=jax.tree.map(lambda _: vmem(), outs),
        compiler_params=pltpu.CompilerParams(vmem_limit_bytes=VMEM_LIMIT),
        name=name,
    )


def f32(*shape):
    return jax.ShapeDtypeStruct(shape, jnp.float32)


def pack_rows(group, rhs, cr, cc, lk, agg, m, w_ref, mflat, up, down):
    width = rhs.shape[1]
    pairs = width // 256
    per_row = 3 * pairs
    lane = lax.broadcasted_iota(jnp.int32, (8, LANES), 1)
    row = lax.broadcasted_iota(jnp.int32, (8, LANES), 0)
    for j in range(pairs):
        base = (row * pairs + j) * 256
        p1 = agg[pl.ds(3 * j + 1, 8, stride=per_row), :]
        p2 = agg[pl.ds(3 * j + 2, 8, stride=per_row), :]
        p1 = jnp.broadcast_to(p1[:, 0:1], (8, LANES)) - base
        p2 = jnp.broadcast_to(p2[:, 0:1], (8, LANES)) - base
        s0 = 1.0 / jnp.sqrt(p1.astype(jnp.float32) * float(group))
        s1 = 1.0 / jnp.sqrt((p2 - p1).astype(jnp.float32) * float(group))
        s2 = 1.0 / jnp.sqrt((256 - p2).astype(jnp.float32) * float(group))
        for half in range(2):
            at = lane + half * LANES
            value = jnp.where(at < p1, s0, jnp.where(at < p2, s1, s2))
            w_ref[:, (2 * j + half) * LANES : (2 * j + half + 1) * LANES] = value
    tiles = m.shape[1] // LANES
    for k in range(m.shape[0]):
        for t in range(tiles):
            mflat[k * tiles + t : k * tiles + t + 1, :] = m[k : k + 1, t * LANES : (t + 1) * LANES]
    ncol = width // LANES
    keep = (row == 3).astype(jnp.float32)
    for t in range(ncol):
        s = slice(t * LANES, (t + 1) * LANES)
        a, b, c, d, e = rhs[:, s], lk[:, s], cr[:, s], cc[:, s], w_ref[:, s]
        up[MSG * t : MSG * (t + 1), :] = jnp.concatenate([a[0:5], b[0:5], c[0:5], d[0:5], e[0:4]], axis=0)
        north = keep * pltpu.roll(d, 1, 0)
        b = b + north
        down[MSG * t : MSG * (t + 1), :] = jnp.concatenate([a[3:8], b[3:8], c[3:8], d[3:8], e[4:8]], axis=0)
    half = 2 * tiles
    up[MSG * ncol : MSG * ncol + half, :] = mflat[0:half, :]
    down[MSG * ncol : MSG * ncol + half, :] = mflat[half : 2 * half, :]


def windows(own, above, below):
    zeros = jnp.zeros((3, LANES), jnp.float32)
    out = []
    for i in range(5):
        n = 4 if i == 4 else REACH
        at = 5 * i
        top, low = above[at : at + n], below[at : at + n]
        pad = jnp.zeros((8 - n, LANES), jnp.float32)
        out.append(jnp.concatenate([pad, top, own[i], low, pad], axis=0))
    return out


def pack_cols(rhs, cr, cc, lk, w, mflat, above, below, left, right):
    ncol = rhs.shape[1] // LANES
    half = mflat.shape[0] // 2
    for t, out in ((0, left), (ncol - 1, right)):
        s = slice(t * LANES, (t + 1) * LANES)
        own = [r[:, s] for r in (rhs, lk, cr, cc, w)]
        rows = slice(MSG * t, MSG * (t + 1))
        for i, value in enumerate(windows(own, above[rows, :], below[rows, :])):
            out[WROWS * i : WROWS * (i + 1), :] = value
        at = 5 * WROWS
        out[at : at + half, :] = above[MSG * ncol : MSG * ncol + half, :]
        out[at + half : at + 3 * half, :] = mflat[...]
        out[at + 3 * half : at + 4 * half, :] = below[MSG * ncol : MSG * ncol + half, :]


def shifted(v):
    n = v.shape[1]
    r = v.shape[0]
    return (pltpu.roll(v, n - 1, 1), pltpu.roll(v, 1, 1), pltpu.roll(v, r - 1, 0), pltpu.roll(v, 1, 0))


def scaled_apply(v, east, west, south, north):
    e, w, s, n = shifted(v)
    return v - east * e - west * w - south * s - north * n


def middle(zsize, rhs, cr, cc, lk, w, above, below, left, right, pre_o, z_o, w_o, east_o, west_o, south_o, north_o, msg):
    width = rhs.shape[1]
    ncol = width // LANES
    pieces = [[left[WROWS * i : WROWS * (i + 1), :]] for i in range(5)]
    for t in range(ncol):
        s = slice(t * LANES, (t + 1) * LANES)
        own = [r[:, s] for r in (rhs, lk, cr, cc, w)]
        rows = slice(MSG * t, MSG * (t + 1))
        for i, value in enumerate(windows(own, above[rows, :], below[rows, :])):
            pieces[i].append(value)
    for i in range(5):
        pieces[i].append(right[WROWS * i : WROWS * (i + 1), :])
    b, l, r, c, wt = [jnp.concatenate(p, axis=1) for p in pieces]
    n = b.shape[1]
    rw, cn = pltpu.roll(r, 1, 1), pltpu.roll(c, 1, 0)
    diag = l + r + c + rw + cn
    inside = l > 0.0
    inv = jnp.where(inside, 1.0 / jnp.where(inside, diag, 1.0), 0.0)
    east, west, south, north = r * inv, rw * inv, c * inv, cn * inv
    op = functools.partial(scaled_apply, east=east, west=west, south=south, north=north)
    z = b * inv
    d = z * (1.0 / THETA)
    x = d
    z = z - op(d)
    d = (RHO1 * RHO0) * d + (2.0 * RHO1 / DELTA) * z
    x = x + d
    z = z - op(d)
    d = (RHO2 * RHO1) * d + (2.0 * RHO2 / DELTA) * z
    x = x + d
    z = z - op(d)
    g = wt * diag * (z - OMEGA * op(z))
    pre_o[...] = x
    z_o[...] = z
    w_o[...] = wt
    east_o[...] = east
    west_o[...] = west
    south_o[...] = south
    north_o[...] = north
    part = g[8:16, LANES : 2 * LANES]
    for t in range(2, ncol + 1):
        part = part + g[8:16, t * LANES : (t + 1) * LANES]
    total = jnp.sum(part, axis=1, keepdims=True)
    place = (lax.axis_index("z") * 2 + lax.axis_index("core")) * 4
    lane = lax.broadcasted_iota(jnp.int32, (8, LANES), 1)
    row = lax.broadcasted_iota(jnp.int32, (8, LANES), 0)
    spread = jnp.where(lane == lax.rem(place, LANES) + row // 2, total, 0.0)
    line = jnp.sum(spread, axis=0, keepdims=True)
    rows = lax.broadcasted_iota(jnp.int32, (msg.shape[1], LANES), 0)
    msg[...] = jnp.broadcast_to(jnp.where(rows == place // LANES, line, 0.0)[None], msg.shape)


def last(xs, gathered, mflat, above, below, left, right, pre, z_i, wt, east, west, south, north, out):
    ncol = out.shape[1] // LANES
    ncols = lax.axis_size("cols")
    tiles = mflat.shape[0] // 4
    half = 2 * tiles
    at = 5 * WROWS
    own_m = [above[MSG * ncol + tiles * k : MSG * ncol + tiles * (k + 1), :] for k in range(2)]
    own_m += [mflat[tiles * k : tiles * (k + 1), :] for k in range(4)]
    own_m += [below[MSG * ncol + tiles * k : MSG * ncol + tiles * (k + 1), :] for k in range(2)]
    left_m = [left[at + tiles * k : at + tiles * (k + 1), :] for k in range(8)]
    right_m = [right[at + tiles * k : at + tiles * (k + 1), :] for k in range(8)]
    me = lax.axis_index("cols")
    blank = jnp.zeros((4, LANES), jnp.float32)

    def corrections(group, mats):
        v = []
        for x in range(xs):
            v.append(gathered[(2 * x) * ncols + group] + gathered[(2 * x + 1) * ncols + group])
        v = jnp.concatenate(v, axis=0)
        lines = [blank]
        for m in mats:
            p = jnp.sum(m * v, axis=0, keepdims=True)
            lines += [p, p]
        lines.append(blank)
        return jnp.sum(jnp.concatenate(lines, axis=0), axis=1, keepdims=True)

    cl = corrections(jnp.maximum(me - 1, 0), left_m)
    co = corrections(me, own_m)
    cn = corrections(jnp.minimum(me + 1, ncols - 1), right_m)
    w = wt[...]
    n = w.shape[1]
    lane = lax.broadcasted_iota(jnp.int32, (1, n), 1)
    lifted = w * jnp.where(lane < LANES, cl, jnp.where(lane >= n - LANES, cn, co))
    op = functools.partial(scaled_apply, east=east[...], west=west[...], south=south[...], north=north[...])
    e = lifted - OMEGA * op(lifted)
    x = pre[...] + e
    z = z_i[...] - op(e)
    d = z * (1.0 / THETA)
    x = x + d
    z = z - op(d)
    d = (RHO1 * RHO0) * d + (2.0 * RHO1 / DELTA) * z
    x = x + d
    z = z - op(d)
    d = (RHO2 * RHO1) * d + (2.0 * RHO2 / DELTA) * z
    x = x + d
    out[...] = x[8:16, LANES : n - LANES]


def local(sizes, rhs, cond_row, cond_col, leak, agg_members, coarse_inverse):
    xs, zs, cores, cols = sizes
    width = rhs.shape[1]
    ncol = width // LANES
    m = coarse_inverse[0]
    tiles = m.shape[1] // LANES
    group = agg_members.shape[2] // 4
    agg = agg_members[0, 0]
    length = MSG * ncol + 2 * tiles
    w, mflat, up, down = call(
        functools.partial(pack_rows, group),
        [f32(8, width), f32(4 * tiles, LANES), f32(length, LANES), f32(length, LANES)],
        6,
        "pack_rows",
    )(rhs, cond_row, cond_col, leak, agg, m)
    devices = xs * zs * cores
    ahead = [(i, i + 1) for i in range(devices - 1)]
    back = [(j, i) for i, j in ahead]
    above = lax.ppermute(down, ROWAX, ahead)
    below = lax.ppermute(up, ROWAX, back)
    edge = f32(5 * WROWS + 8 * tiles, LANES)
    to_left, to_right = call(pack_cols, [edge, edge], 8, "pack_cols")(
        rhs, cond_row, cond_col, leak, w, mflat, above, below
    )
    ahead = [(i, i + 1) for i in range(cols - 1)]
    back = [(j, i) for i, j in ahead]
    left = lax.ppermute(to_right, "cols", ahead)
    right = lax.ppermute(to_left, "cols", back)
    per_x = max(1, zs * cores * 4 // LANES)
    win = f32(WROWS, width + 2 * LANES)
    pre, z, wt, east, west, south, north, msg = call(
        functools.partial(middle, zs), [win] * 7 + [f32(zs, per_x, LANES)], 9, "middle"
    )(rhs, cond_row, cond_col, leak, w, above, below, left, right)
    got = lax.all_to_all(msg, "z", 0, 0, tiled=True)
    line = jnp.sum(got, axis=0)
    second = jnp.broadcast_to(line[None], (xs * cores * cols, per_x, LANES))
    gathered = lax.all_to_all(second, ("x", "core", "cols"), 0, 0, tiled=True)
    return call(functools.partial(last, xs), f32(8, width), 13, "last")(
        gathered, mflat, above, below, left, right, pre, z, wt, east, west, south, north
    )


def solution(mesh):
    rows, cols = mesh.shape["rows"], mesh.shape["cols"]
    cores = 2
    xs = 4 if rows == 256 else 2
    zs = rows // (xs * cores)
    fine = Mesh(mesh.devices.reshape(xs, zs, cores, cols), ("x", "z", "core", "cols"))
    spec = P(ROWAX, "cols")
    in_specs = (spec, spec, spec, spec, P(ROWAX, "cols", None, None), P("cols", ROWAX, None))
    return jax.shard_map(
        functools.partial(local, (xs, zs, cores, cols)),
        mesh=fine,
        in_specs=in_specs,
        out_specs=spec,
        check_vma=False,
    )
```

time: 638 us -> 95.2 us (0.15)
  blocking collectives: 501 us -> 61.4 us
  starting transfers between devices: 94.8 us -> 20 us
  waiting for transfers between devices: 30.5 us -> 5.57 us
    unnamed x1 -> x0, blocking collectives: 501 us -> none
    ppermute x34 -> x4, starting transfers between devices: 94.8 us -> 20 us  [the longest x1 12.4 us: local(): below = lax.ppermute(up, ROWAX, back)]
    all_to_all x0 -> x2, blocking collectives: none -> 61.4 us  [the longest x1 45.1 us: local(): got = lax.all_to_all(msg, 'z', 0, 0, tiled=True)]
    ppermute x34 -> x4, waiting for transfers between devices: 30.5 us -> 5.57 us  [the longest x1 3.8 us: local(): right = lax.ppermute(to_left, 'cols', back)]
  transfers between devices with their start and end apart: 34 -> 4, of which waited for: 18 -> 3; matrix products, arithmetic and copies ran while one was open for 0% -> 0% of each run, Pallas kernels for 0% -> 0%
where the time goes in v1:
time: 95.2 us; the launch traced here: 94.7 us
  blocking collectives  61.4 us (64%)
  starting transfers between devices  20 us (21%)
  waiting for transfers between devices  5.57 us (6%)
  local copies, waits for them, and re-layouts  4.98 us (5%)
  Pallas kernels  2.67 us (3%)
    all_to_all x1, blocking collectives, local(): got = lax.all_to_all(msg, 'z', 0, 0, tiled=True)  45.1 us
    all_to_all x1, blocking collectives, local(): gathered = lax.all_to_all(second, ('x', 'core', 'cols'), 0, 0, tiled=True)  16.3 us
    ppermute x1, starting transfers between devices, local(): below = lax.ppermute(up, ROWAX, back)  12.4 us
    unnamed x12, local copies, waits for them, and re-layouts  4.96 us
    ppermute x1, starting transfers between devices, local(): above = lax.ppermute(down, ROWAX, ahead)  4.94 us
    ppermute x1, waiting for transfers between devices, local(): right = lax.ppermute(to_left, 'cols', back)  3.8 us
  transfers between devices with their start and end apart: 4, of which 3 were waited for; matrix products, arithmetic and copies ran while one was open for 0% of the time, Pallas kernels for 0%

profile of v1, /device:TPU:1, one launch (start us, length us, event | category | flops | bytes accessed | tf_op | source)
XLA Modules:
  0.0 94.7 jit_solution(13988905846865378773)
XLA Ops:
  0.0 0.0 copy-start
  0.0 0.8 copy-done
  0.8 0.0 copy-start.1
  0.8 0.8 copy-done.1
  1.7 0.0 copy-start.2
  1.7 0.8 copy-done.2
  2.5 0.0 copy-start.3
  2.5 0.8 copy-done.3
  3.4 0.0 copy-start.4
  3.4 0.9 copy-done.4
  4.3 0.7 copy-done.5
  5.0 0.1 pack_rows.1
  5.1 4.9 %collective-permute-start = (f32[400,128]{1,0:T(8,128)S(1)}, f32[400,128]{1,0:T(8,128)S(1)}, u32[]{:S(2)}, u32[]{:S(2)}) collective-permute-start(f32[400,128]{1,0:T(8,128)S(1)} %get-tuple-element.20), channel_id=1, source_target_pairs={{0,4},{4,8},{8,12},{12,16},{16,20},{20,24},{24,28},{28,32},{32,36}... | collective-permute-start | bytes 614408 | tf_op jit(solution)/shard_map/ppermute | solution.py:236
  10.1 12.4 %collective-permute-start.1 = (f32[400,128]{1,0:T(8,128)S(1)}, f32[400,128]{1,0:T(8,128)S(1)}, u32[]{:S(2)}, u32[]{:S(2)}) collective-permute-start(f32[400,128]{1,0:T(8,128)S(1)} %get-tuple-element.21), channel_id=1, source_target_pairs={{4,0},{8,4},{12,8},{16,12},{20,16},{24,20},{28,24},{32,28},{36,32}... | collective-permute-start | bytes 614408 | tf_op jit(solution)/shard_map/ppermute | solution.py:237
  22.5 0.0 collective-permute-done.above
  22.5 1.0 %collective-permute-done.1.below = f32[400,128]{1,0:T(8,128)S(1)} collective-permute-done((f32[400,128]{1,0:T(8,128)S(1)}, f32[400,128]{1,0:T(8,128)S(1)}, u32[]{:S(2)}, u32[]{:S(2)}) %collective-permute-start.1) | collective-permute-done | bytes 204832 | tf_op jit(solution)/shard_map/ppermute | solution.py:237
  23.6 1.3 %collective-permute-start.2 = (f32[184,128]{1,0:T(8,128)S(1)}, f32[184,128]{1,0:T(8,128)S(1)}, u32[]{:S(2)}, u32[]{:S(2)}) collective-permute-start(f32[184,128]{1,0:T(8,128)S(1)} %get-tuple-element.23), channel_id=1, source_target_pairs={{0,1},{1,2},{2,3},{4,5},{5,6},{6,7},{8,9},{9,10},{10,11},{12,13},{... | collective-permute-start | bytes 282632 | tf_op jit(solution)/shard_map/ppermute | solution.py:244
  24.9 1.3 %collective-permute-start.3 = (f32[184,128]{1,0:T(8,128)S(1)}, f32[184,128]{1,0:T(8,128)S(1)}, u32[]{:S(2)}, u32[]{:S(2)}) collective-permute-start(f32[184,128]{1,0:T(8,128)S(1)} %get-tuple-element.24), channel_id=1, source_target_pairs={{1,0},{2,1},{3,2},{5,4},{6,5},{7,6},{9,8},{10,9},{11,10},{13,12},{... | collective-permute-start | bytes 282632 | tf_op jit(solution)/shard_map/ppermute | solution.py:245
  26.2 0.7 collective-permute-done.2.left
  26.9 3.8 %collective-permute-done.3.right = f32[184,128]{1,0:T(8,128)S(1)} collective-permute-done((f32[184,128]{1,0:T(8,128)S(1)}, f32[184,128]{1,0:T(8,128)S(1)}, u32[]{:S(2)}, u32[]{:S(2)}) %collective-permute-start.3) | collective-permute-done | bytes 94240 | tf_op jit(solution)/shard_map/ppermute | solution.py:245
  30.7 1.1 %middle.1 = (f32[24,2304]{1,0:T(8,128)S(1)}, f32[24,2304]{1,0:T(8,128)S(1)}, f32[24,2304]{1,0:T(8,128)S(1)}, f32[24,2304]{1,0:T(8,128)S(1)}, f32[24,2304]{1,0:T(...) custom-call(f32[8,2048]{1,0:T(8,128)S(1)} %copy-done, ...), custom_call_target="tpu_custom_call" | custom-call | tf_op jit(solution)/shard_map/middle/pallas_call | solution.py:248
  31.8 45.1 %all_to_all.10 = f32[32,2,128]{2,1,0:T(2,128)S(1)} all-to-all(f32[32,2,128]{2,1,0:T(2,128)S(1)} %get-tuple-element.25), channel_id=1, replica_groups=mesh['x'=4,'z'=32,'core'=2,'cols'=4] {'z'}, dimensions={0} | all-to-all | bytes 65536 | tf_op jit(solution)/shard_map/all_to_all | solution.py:251
  76.9 16.3 %all_to_all.11.gathered = f32[32,2,128]{2,1,0:T(2,128)S(1)} all-to-all(f32[32,2,128]{2,1,0:T(2,128)S(1)} %broadcast_in_dim.2), channel_id=1, replica_groups=mesh['x'=4,'z'=32,'core'=2,'cols'=4] {'x','core','cols'}, dimensions={0} | all-to-all | bytes 65536 | tf_op jit(solution)/shard_map/all_to_all | solution.py:254
  93.3 1.5 %last.1 = f32[8,2048]{1,0:T(8,128)} custom-call(f32[32,2,128]{2,1,0:T(2,128)S(1)} %all_to_all.11.gathered, f32[32,128]{1,0:T(8,128)S(1)} %get-tuple-element.22.mflat, f32[400,128]{1,0:T(8,128)S(1)} %collective-permute-done.above, f32[400,128]{1,0:T(8,128)S(1)} %collective-permute-done.1.below, f32[184,128]{1,0:T(8,128)S(1)} %collective-permute-done.2.left, ...), custom_call_target="tpu_custom_call" | custom-call | tf_op jit(solution)/shard_map/last/pallas_call | solution.py:255
  (4 shorter events, 0.1 us)
Async XLA Ops:
  0.0 0.8 copy-start
  0.8 0.8 copy-start.1
  1.7 0.8 copy-start.2
  2.5 0.8 copy-start.3
  3.4 0.9 copy-start.4
  4.3 0.7 copy-start.5
  5.1 17.4 %collective-permute-start = (f32[400,128]{1,0:T(8,128)S(1)}, f32[400,128]{1,0:T(8,128)S(1)}, u32[]{:S(2)}, u32[]{:S(2)}) collective-permute-start(f32[400,128]{1,0:T(8,128)S(1)} %get-tuple-element.20), channel_id=1, source_target_pairs={{0,4},{4,8},{8,12},{12,16},{16,20},{20,24},{24,28},{28,32},{32,36}... | collective-permute-start | bytes 614408 | tf_op jit(solution)/shard_map/ppermute | solution.py:236
  10.1 13.5 %collective-permute-start.1 = (f32[400,128]{1,0:T(8,128)S(1)}, f32[400,128]{1,0:T(8,128)S(1)}, u32[]{:S(2)}, u32[]{:S(2)}) collective-permute-start(f32[400,128]{1,0:T(8,128)S(1)} %get-tuple-element.21), channel_id=1, source_target_pairs={{4,0},{8,4},{12,8},{16,12},{20,16},{24,20},{28,24},{32,28},{36,32}... | collective-permute-start | bytes 614408 | tf_op jit(solution)/shard_map/ppermute | solution.py:237
  23.6 3.3 %collective-permute-start.2 = (f32[184,128]{1,0:T(8,128)S(1)}, f32[184,128]{1,0:T(8,128)S(1)}, u32[]{:S(2)}, u32[]{:S(2)}) collective-permute-start(f32[184,128]{1,0:T(8,128)S(1)} %get-tuple-element.23), channel_id=1, source_target_pairs={{0,1},{1,2},{2,3},{4,5},{5,6},{6,7},{8,9},{9,10},{10,11},{12,13},{... | collective-permute-start | bytes 282632 | tf_op jit(solution)/shard_map/ppermute | solution.py:244
  24.9 5.8 %collective-permute-start.3 = (f32[184,128]{1,0:T(8,128)S(1)}, f32[184,128]{1,0:T(8,128)S(1)}, u32[]{:S(2)}, u32[]{:S(2)}) collective-permute-start(f32[184,128]{1,0:T(8,128)S(1)} %get-tuple-element.24), channel_id=1, source_target_pairs={{1,0},{2,1},{3,2},{5,4},{6,5},{7,6},{9,8},{10,9},{11,10},{13,12},{... | collective-permute-start | bytes 282632 | tf_op jit(solution)/shard_map/ppermute | solution.py:245

commit v2 on v1

v2 whole, which is shorter than its diff:
```python
import functools

import jax
import jax.numpy as jnp
from jax import lax
from jax.experimental import pallas as pl
from jax.experimental.pallas import tpu as pltpu
from jax.sharding import Mesh
from jax.sharding import PartitionSpec as P

THETA = 1.05
DELTA = 0.95
OMEGA = 2.0 / 3.0
RHO0 = DELTA / THETA
RHO1 = 1.0 / (2.0 * THETA / DELTA - RHO0)
RHO2 = 1.0 / (2.0 * THETA / DELTA - RHO1)
LANES = 128
REACH = 5
WROWS = 24
MSG = 24
ROWAX = ("x", "z", "core")
VMEM_LIMIT = 48 * 1024 * 1024
FIRST_LIMIT = 61 * 1024 * 1024


def call(kernel, outs, nin, name, space=pltpu.VMEM, scratch=(), limit=VMEM_LIMIT):
    return pl.pallas_call(
        kernel,
        out_shape=outs,
        in_specs=[pl.BlockSpec(memory_space=space)] * nin,
        out_specs=jax.tree.map(lambda _: pl.BlockSpec(memory_space=pltpu.VMEM), outs),
        scratch_shapes=scratch,
        compiler_params=pltpu.CompilerParams(vmem_limit_bytes=limit),
        name=name,
    )


def f32(*shape):
    return jax.ShapeDtypeStruct(shape, jnp.float32)


def weights(group, agg, w_ref):
    pairs = w_ref.shape[1] // 256
    per_row = 3 * pairs
    lane = lax.broadcasted_iota(jnp.int32, (8, LANES), 1)
    row = lax.broadcasted_iota(jnp.int32, (8, LANES), 0)
    for j in range(pairs):
        base = (row * pairs + j) * 256
        p1 = agg[pl.ds(3 * j + 1, 8, stride=per_row), :]
        p2 = agg[pl.ds(3 * j + 2, 8, stride=per_row), :]
        p1 = jnp.broadcast_to(p1[:, 0:1], (8, LANES)) - base
        p2 = jnp.broadcast_to(p2[:, 0:1], (8, LANES)) - base
        s0 = 1.0 / jnp.sqrt(p1.astype(jnp.float32) * float(group))
        s1 = 1.0 / jnp.sqrt((p2 - p1).astype(jnp.float32) * float(group))
        s2 = 1.0 / jnp.sqrt((256 - p2).astype(jnp.float32) * float(group))
        for half in range(2):
            at = lane + half * LANES
            value = jnp.where(at < p1, s0, jnp.where(at < p2, s1, s2))
            w_ref[:, (2 * j + half) * LANES : (2 * j + half + 1) * LANES] = value


def halo_rows(fields, downward):
    b, l, r, c, w = fields
    row = lax.broadcasted_iota(jnp.int32, (8, LANES), 0)
    first = jnp.concatenate([b[0:5], l[0:5], r[0:5], c[0:5], w[0:4]], axis=0)
    l = l + jnp.where(row == 3, pltpu.roll(c, 1, 0), 0.0)
    final = jnp.concatenate([b[3:8], l[3:8], r[3:8], c[3:8], w[4:8]], axis=0)
    return jnp.where(downward, final, first)


def first_kernel(group, rhs, cr, cc, lk, agg, m, w_o, mflat, core_msg, edges, b_v, r_v, c_v, l_v, agg_v, m_v, sems):
    copies = []
    for i, (src, dst) in enumerate(((agg, agg_v), (m, m_v), (rhs, b_v), (cr, r_v), (cc, c_v), (lk, l_v))):
        copies.append(pltpu.make_async_copy(src, dst, sems.at[i]))
    for copy in copies:
        copy.start()
    for copy in copies:
        copy.wait()
    weights(group, agg_v, w_o)
    tiles = m.shape[1] // LANES
    for k in range(4):
        for t in range(tiles):
            mflat[k * tiles + t : k * tiles + t + 1, :] = m_v[k : k + 1, t * LANES : (t + 1) * LANES]
    downward = lax.axis_index("core") == 0
    ncol = w_o.shape[1] // LANES
    refs = (b_v, l_v, r_v, c_v, w_o)
    for t in range(ncol):
        own = [r[:, t * LANES : (t + 1) * LANES] for r in refs]
        core_msg[MSG * t : MSG * (t + 1), :] = halo_rows(own, downward)
    half = 2 * tiles
    core_msg[MSG * ncol :, :] = jnp.where(downward, mflat[half:, :], mflat[:half, :])
    me = lax.axis_index("cols")
    cols = lax.axis_size("cols")
    n = w_o.shape[1]
    mine = mflat[...]
    left = jnp.concatenate([r[:, 0:LANES] for r in refs] + [mine], axis=0)
    right = jnp.concatenate([r[:, n - LANES : n] for r in refs] + [mine], axis=0)
    for c in range(cols):
        value = jnp.where(me > c, left, right)
        edges[c] = value
        edges[cols + c] = value


def side_block(got, core, step):
    cols = lax.axis_size("cols")
    c = lax.axis_index("cols") + step
    ok = jnp.logical_and(c >= 0, c < cols)
    return jnp.where(ok, got[core * cols + jnp.clip(c, 0, cols - 1)], 0.0)


def chip_kernel(b, r, c, l, w, mflat, got, s1, msg):
    core = lax.axis_index("core")
    downward = core == 1
    refs = (b, l, r, c, w)
    ncol = b.shape[1] // LANES
    half = mflat.shape[0] // 2
    lb, rb = side_block(got, core, -1), side_block(got, core, 1)
    columns = [[lb[8 * i : 8 * i + 8] for i in range(5)]]
    columns += [[x[:, t * LANES : (t + 1) * LANES] for x in refs] for t in range(ncol)]
    columns.append([rb[8 * i : 8 * i + 8] for i in range(5)])
    for t, fields in enumerate(columns):
        msg[MSG * t : MSG * (t + 1), :] = halo_rows(fields, downward)
    at = MSG * (ncol + 2)
    for i, mats in enumerate((lb[40:], mflat[...], rb[40:])):
        msg[at + half * i : at + half * (i + 1), :] = jnp.where(downward, mats[half:], mats[:half])


def unpacked(rows, top):
    out = []
    for i in range(5):
        n = 4 if i == 4 else REACH
        pad = jnp.zeros((8 - n, LANES), jnp.float32)
        piece = rows[5 * i : 5 * i + n]
        out.append(jnp.concatenate([pad, piece] if top else [piece, pad], axis=0))
    return out


def shifted(v):
    n = v.shape[1]
    r = v.shape[0]
    return (pltpu.roll(v, n - 1, 1), pltpu.roll(v, 1, 1), pltpu.roll(v, r - 1, 0), pltpu.roll(v, 1, 0))


def scaled_apply(v, east, west, south, north):
    e, w, s, n = shifted(v)
    return v - east * e - west * w - south * s - north * n


def middle(bf, rf, cf, lf, w, mflat, got, s1, s2, pre_o, z_o, w_o, east_o, west_o, south_o, north_o, mwin, msg):
    width = bf.shape[1]
    ncol = width // LANES
    core = lax.axis_index("core")
    upper = core == 0
    refs = (bf, lf, rf, cf, w)
    half = mflat.shape[0] // 2
    pieces = [[] for _ in range(5)]
    mats = []
    for t in range(ncol + 2):
        chip = s2[MSG * t : MSG * (t + 1), :]
        if 0 < t <= ncol:
            own = [x[:, (t - 1) * LANES : t * LANES] for x in refs]
            pair = s1[MSG * (t - 1) : MSG * t, :]
            above = unpacked(jnp.where(upper, chip, pair), True)
            below = unpacked(jnp.where(upper, pair, chip), False)
        else:
            step = -1 if t == 0 else 1
            block = side_block(got, core, step)
            pair = side_block(got, 1 - core, step)
            own = [block[8 * i : 8 * i + 8] for i in range(5)]
            near = [pair[8 * i : 8 * i + 8] for i in range(5)]
            above = [jnp.where(upper, a, e) for a, e in zip(unpacked(chip, True), near)]
            below = [jnp.where(upper, e, a) for a, e in zip(unpacked(chip, False), near)]
            mats.append((block[40:], jnp.where(upper, pair[40 : 40 + half], pair[40 + half :])))
        for i in range(5):
            pieces[i].append(jnp.concatenate([above[i], own[i], below[i]], axis=0))
    mats.insert(1, (mflat[...], s1[MSG * ncol :, :]))
    at = MSG * (ncol + 2)
    for i, (mine, pair) in enumerate(mats):
        chip = s2[at + half * i : at + half * (i + 1), :]
        mwin[4 * half * i : 4 * half * i + half, :] = jnp.where(upper, chip, pair)
        mwin[4 * half * i + half : 4 * half * i + 3 * half, :] = mine
        mwin[4 * half * i + 3 * half : 4 * half * (i + 1), :] = jnp.where(upper, pair, chip)
    b, l, r, c, wt = [jnp.concatenate(p, axis=1) for p in pieces]
    n = b.shape[1]
    rw, cn = pltpu.roll(r, 1, 1), pltpu.roll(c, 1, 0)
    diag = l + r + c + rw + cn
    inside = l > 0.0
    inv = jnp.where(inside, 1.0 / jnp.where(inside, diag, 1.0), 0.0)
    east, west, south, north = r * inv, rw * inv, c * inv, cn * inv
    op = functools.partial(scaled_apply, east=east, west=west, south=south, north=north)
    z = b * inv
    d = z * (1.0 / THETA)
    x = d
    z = z - op(d)
    d = (RHO1 * RHO0) * d + (2.0 * RHO1 / DELTA) * z
    x = x + d
    z = z - op(d)
    d = (RHO2 * RHO1) * d + (2.0 * RHO2 / DELTA) * z
    x = x + d
    z = z - op(d)
    g = wt * diag * (z - OMEGA * op(z))
    pre_o[...] = x
    z_o[...] = z
    w_o[...] = wt
    east_o[...] = east
    west_o[...] = west
    south_o[...] = south
    north_o[...] = north
    part = g[8:16, LANES : 2 * LANES]
    for t in range(2, ncol + 1):
        part = part + g[8:16, t * LANES : (t + 1) * LANES]
    total = jnp.sum(part, axis=1, keepdims=True)
    place = (lax.axis_index("z") * 2 + lax.axis_index("core")) * 4
    lane = lax.broadcasted_iota(jnp.int32, (8, LANES), 1)
    row = lax.broadcasted_iota(jnp.int32, (8, LANES), 0)
    spread = jnp.where(lane == lax.rem(place, LANES) + row // 2, total, 0.0)
    line = jnp.sum(spread, axis=0, keepdims=True)
    rows = lax.broadcasted_iota(jnp.int32, (msg.shape[1], LANES), 0)
    msg[...] = jnp.broadcast_to(jnp.where(rows == place // LANES, line, 0.0)[None], msg.shape)


def last(xs, gathered, mwin, pre, z_i, wt, east, west, south, north, out):
    ncols = lax.axis_size("cols")
    tiles = mwin.shape[0] // 24
    mats = [[mwin[tiles * (8 * g + k) : tiles * (8 * g + k + 1), :] for k in range(8)] for g in range(3)]
    me = lax.axis_index("cols")
    blank = jnp.zeros((4, LANES), jnp.float32)

    def corrections(group, mats):
        v = []
        for x in range(xs):
            v.append(gathered[(2 * x) * ncols + group] + gathered[(2 * x + 1) * ncols + group])
        v = jnp.concatenate(v, axis=0)
        lines = [blank]
        for m in mats:
            p = jnp.sum(m * v, axis=0, keepdims=True)
            lines += [p, p]
        lines.append(blank)
        return jnp.sum(jnp.concatenate(lines, axis=0), axis=1, keepdims=True)

    cl = corrections(jnp.maximum(me - 1, 0), mats[0])
    co = corrections(me, mats[1])
    cn = corrections(jnp.minimum(me + 1, ncols - 1), mats[2])
    w = wt[...]
    n = w.shape[1]
    lane = lax.broadcasted_iota(jnp.int32, (1, n), 1)
    lifted = w * jnp.where(lane < LANES, cl, jnp.where(lane >= n - LANES, cn, co))
    op = functools.partial(scaled_apply, east=east[...], west=west[...], south=south[...], north=north[...])
    e = lifted - OMEGA * op(lifted)
    x = pre[...] + e
    z = z_i[...] - op(e)
    d = z * (1.0 / THETA)
    x = x + d
    z = z - op(d)
    d = (RHO1 * RHO0) * d + (2.0 * RHO1 / DELTA) * z
    x = x + d
    z = z - op(d)
    d = (RHO2 * RHO1) * d + (2.0 * RHO2 / DELTA) * z
    x = x + d
    out[...] = x[8:16, LANES : n - LANES]


def local(sizes, rhs, cond_row, cond_col, leak, agg_members, coarse_inverse):
    xs, zs, cores, cols = sizes
    width = rhs.shape[1]
    ncol = width // LANES
    m = coarse_inverse[0]
    tiles = m.shape[1] // LANES
    group = agg_members.shape[2] // 4
    agg = agg_members[0, 0]
    block = f32(8, width)
    edge = 40 + 4 * tiles
    w, mflat, core_msg, edges = call(
        functools.partial(first_kernel, group),
        [block, f32(4 * tiles, LANES), f32(MSG * ncol + 2 * tiles, LANES), f32(cores * cols, edge, LANES)],
        6,
        "first",
        space=pltpu.HBM,
        limit=FIRST_LIMIT,
        scratch=[pltpu.VMEM((8, width), jnp.float32)] * 4
        + [
            pltpu.VMEM(agg.shape, jnp.int32),
            pltpu.VMEM(m.shape, jnp.float32),
            pltpu.SemaphoreType.DMA((6,)),
        ],
    )(rhs, cond_row, cond_col, leak, agg, m)
    b, r, c, l = rhs, cond_row, cond_col, leak
    s1 = lax.ppermute(core_msg, "core", [(0, 1), (1, 0)])
    got = lax.all_to_all(edges, ("core", "cols"), 0, 0, tiled=True)
    chip_msg = call(chip_kernel, f32(MSG * (ncol + 2) + 6 * tiles, LANES), 8, "chip")(
        b, r, c, l, w, mflat, got, s1
    )
    devices = xs * zs * cores
    swap = []
    for i in range(1, devices - 1, 2):
        swap += [(i, i + 1), (i + 1, i)]
    s2 = lax.ppermute(chip_msg, ROWAX, swap)
    per_x = max(1, zs * cores * 4 // LANES)
    win = f32(WROWS, width + 2 * LANES)
    pre, z, wt, east, west, south, north, mwin, msg = call(
        middle, [win] * 7 + [f32(24 * tiles, LANES), f32(zs, per_x, LANES)], 9, "middle"
    )(b, r, c, l, w, mflat, got, s1, s2)
    spread = lax.all_to_all(msg, "z", 0, 0, tiled=True)
    line = jnp.sum(spread, axis=0)
    second = jnp.broadcast_to(line[None], (xs * cores * cols, per_x, LANES))
    gathered = lax.all_to_all(second, ("x", "core", "cols"), 0, 0, tiled=True)
    return call(functools.partial(last, xs), block, 9, "last")(
        gathered, mwin, pre, z, wt, east, west, south, north
    )


def solution(mesh):
    rows, cols = mesh.shape["rows"], mesh.shape["cols"]
    cores = 2
    xs = 4 if rows == 256 else 2
    zs = rows // (xs * cores)
    fine = Mesh(mesh.devices.reshape(xs, zs, cores, cols), ("x", "z", "core", "cols"))
    spec = P(ROWAX, "cols")
    in_specs = (spec, spec, spec, spec, P(ROWAX, "cols", None, None), P("cols", ROWAX, None))
    return jax.shard_map(
        functools.partial(local, (xs, zs, cores, cols)),
        mesh=fine,
        in_specs=in_specs,
        out_specs=spec,
        check_vma=False,
    )
```

time: 95.2 us -> 91.6 us (0.962)
  blocking collectives: 61.4 us -> 54.4 us
  local copies, waits for them, and re-layouts: 4.98 us -> 0.05 us
  waiting for transfers between devices: 5.57 us -> 10.5 us
  Pallas kernels: 2.67 us -> 4.59 us
  starting transfers between devices: 20 us -> 21.6 us
    all_to_all x0 -> x1, starting transfers between devices: none -> 17.6 us  [local(): got = lax.all_to_all(edges, ('core', 'cols'), 0, 0, tiled=True)]
    ppermute x4 -> x2, starting transfers between devices: 20 us -> 3.92 us  [the longest x1 2 us: local(): s1 = lax.ppermute(core_msg, 'core', [(0, 1), (1, 0)])]
    all_to_all x1, blocking collectives: 45.1 us -> 39 us  [local(): spread = lax.all_to_all(msg, 'z', 0, 0, tiled=True)]
    unnamed x12 -> x14, local copies, waits for them, and re-layouts: 4.96 us -> 0.04 us
    all_to_all x0 -> x1, waiting for transfers between devices: none -> 3.57 us  [local(): got = lax.all_to_all(edges, ('core', 'cols'), 0, 0, tiled=True)]
    pallas_call x4, Pallas kernels: 2.67 us -> 4.59 us  [the longest x1 2 us: local(): call(functools.partial(first_kernel, group), [block, f32(4 * tiles, LANES...]
    ppermute x4 -> x2, waiting for transfers between devices: 5.57 us -> 6.91 us  [the longest x1 5.59 us: local(): s2 = lax.ppermute(chip_msg, ROWAX, swap)]
  transfers between devices with their start and end apart: 4 -> 3, of which waited for: 3 -> 3; matrix products, arithmetic and copies ran while one was open for 0% -> 0% of each run, Pallas kernels for 0% -> 0%
where the time goes in v2:
time: 91.6 us; the launch traced here: 91.3 us
  blocking collectives  54.4 us (59%)
  starting transfers between devices  21.6 us (24%)
  waiting for transfers between devices  10.5 us (11%)
  Pallas kernels  4.59 us (5%)
    all_to_all x1, blocking collectives, local(): spread = lax.all_to_all(msg, 'z', 0, 0, tiled=True)  39 us
    all_to_all x1, starting transfers between devices, local(): got = lax.all_to_all(edges, ('core', 'cols'), 0, 0, tiled=True)  17.6 us
    all_to_all x1, blocking collectives, local(): gathered = lax.all_to_all(second, ('x', 'core', 'cols'), 0, 0, tiled=True)  15.4 us
    ppermute x1, waiting for transfers between devices, local(): s2 = lax.ppermute(chip_msg, ROWAX, swap)  5.59 us
    all_to_all x1, waiting for transfers between devices, local(): got = lax.all_to_all(edges, ('core', 'cols'), 0, 0, tiled=True)  3.57 us
    pallas_call x1, Pallas kernels, local(): call(functools.partial(first_kernel, group), [block, f32(4 * tiles, LANES...  2 us
    ppermute x1, starting transfers between devices, local(): s1 = lax.ppermute(core_msg, 'core', [(0, 1), (1, 0)])  2 us
    ppermute x1, starting transfers between devices, local(): s2 = lax.ppermute(chip_msg, ROWAX, swap)  1.92 us
  transfers between devices with their start and end apart: 3, of which 3 were waited for; matrix products, arithmetic and copies ran while one was open for 0% of the time, Pallas kernels for 0%

profile of v2, /device:TPU:1, one launch (start us, length us, event | category | flops | bytes accessed | tf_op | source)
XLA Modules:
  0.0 91.3 jit_solution(8592210721885684848)
XLA Ops:
  0.0 2.0 %first.1 = (f32[8,2048]{1,0:T(8,128)}, f32[32,128]{1,0:T(8,128)}, f32[400,128]{1,0:T(8,128)}, f32[8,72,128]{2,1,0:T(8,128)}) custom-call(f32[8,2048]{1,0:T(8,128)} %bf.1, f32[8,2048]{1,0:T(8,128)} %rf.1, f32[8,2048]{1,0:T(8,128)} %cf.1, f32[8,2048]{1,0:T(8,128)} %lf.1, s32[192,128]{1,0:T(8,128)} %bitcast.2, f32[4,1024]{1,0:T(4,128)} %bitcast.3), custom_call_target="tpu_custom_call" | custom-call | tf_op jit(solution)/shard_map/first/pallas_call | solution.py:273
  2.0 0.0 copy-start.6
  2.0 0.0 copy-start
  2.0 0.0 copy-start.1
  2.0 0.0 copy-start.2
  2.1 0.0 copy-start.3
  2.1 0.0 copy-start.4
  2.1 0.0 copy-start.5
  2.1 17.6 %all-to-all-start = ((f32[8,72,128]{2,1,0:T(8,128)}), f32[8,72,128]{2,1,0:T(8,128)S(1)}, u32[]{:S(2)}, u32[]{:S(2)}) async-start(f32[8,72,128]{2,1,0:T(8,128)} %get-tuple-element.20), calls=%async_computation | async-start | bytes 589824 | tf_op jit(solution)/shard_map/all_to_all | solution.py:289
  19.7 0.0 copy-done.6
  19.7 2.0 %collective-permute-start = (f32[400,128]{1,0:T(8,128)S(1)}, f32[400,128]{1,0:T(8,128)S(1)}, u32[]{:S(2)}, u32[]{:S(2)}) collective-permute-start(f32[400,128]{1,0:T(8,128)S(1)} %copy-done.6), channel_id=1, source_target_pairs={{0,4},{4,0},{1,5},{5,1},{2,6},{6,2},{3,7},{7,3},{8,12},{12,8},{9,1... | collective-permute-start | bytes 614408 | tf_op jit(solution)/shard_map/ppermute | solution.py:288
  21.7 1.3 %collective-permute-done.s1 = f32[400,128]{1,0:T(8,128)S(1)} collective-permute-done((f32[400,128]{1,0:T(8,128)S(1)}, f32[400,128]{1,0:T(8,128)S(1)}, u32[]{:S(2)}, u32[]{:S(2)}) %collective-permute-start) | collective-permute-done | bytes 204832 | tf_op jit(solution)/shard_map/ppermute | solution.py:288
  23.1 3.6 %all-to-all-done.got = f32[8,72,128]{2,1,0:T(8,128)S(1)} async-done(((f32[8,72,128]{2,1,0:T(8,128)}), f32[8,72,128]{2,1,0:T(8,128)S(1)}, u32[]{:S(2)}, u32[]{:S(2)}) %all-to-all-start) | async-done | bytes 294944 | tf_op jit(solution)/shard_map/all_to_all | solution.py:289
  26.6 0.0 copy-done
  26.7 0.0 copy-done.3
  26.7 0.0 copy-done.4
  26.7 0.0 copy-done.5
  26.7 0.1 chip.1
  26.8 1.9 %collective-permute-start.1 = (f32[480,128]{1,0:T(8,128)S(1)}, f32[480,128]{1,0:T(8,128)S(1)}, u32[]{:S(2)}, u32[]{:S(2)}) collective-permute-start(f32[480,128]{1,0:T(8,128)S(1)} %chip.1), channel_id=1, source_target_pairs={{4,8},{8,4},{12,16},{16,12},{20,24},{24,20},{28,32},{32,28},{36,40... | collective-permute-start | bytes 737288 | tf_op jit(solution)/shard_map/ppermute | solution.py:297
  28.7 5.6 %collective-permute-done.1.s2 = f32[480,128]{1,0:T(8,128)S(1)} collective-permute-done((f32[480,128]{1,0:T(8,128)S(1)}, f32[480,128]{1,0:T(8,128)S(1)}, u32[]{:S(2)}, u32[]{:S(2)}) %collective-permute-start.1) | collective-permute-done | bytes 245792 | tf_op jit(solution)/shard_map/ppermute | solution.py:297
  34.3 1.1 %middle.1 = (f32[24,2304]{1,0:T(8,128)S(1)}, f32[24,2304]{1,0:T(8,128)S(1)}, f32[24,2304]{1,0:T(8,128)S(1)}, f32[24,2304]{1,0:T(8,128)S(1)}, f32[24,2304]{1,0:T(...) custom-call(f32[8,2048]{1,0:T(8,128)S(1)} %copy-done, ...), custom_call_target="tpu_custom_call" | custom-call | tf_op jit(solution)/shard_map/middle/pallas_call | solution.py:300
  35.3 39.0 %all_to_all.15 = f32[32,2,128]{2,1,0:T(2,128)S(1)} all-to-all(f32[32,2,128]{2,1,0:T(2,128)S(1)} %get-tuple-element.22), channel_id=1, replica_groups=mesh['x'=4,'z'=32,'core'=2,'cols'=4] {'z'}, dimensions={0} | all-to-all | bytes 65536 | tf_op jit(solution)/shard_map/all_to_all | solution.py:303
  74.4 15.4 %all_to_all.16.gathered = f32[32,2,128]{2,1,0:T(2,128)S(1)} all-to-all(f32[32,2,128]{2,1,0:T(2,128)S(1)} %broadcast_in_dim.2), channel_id=1, replica_groups=mesh['x'=4,'z'=32,'core'=2,'cols'=4] {'x','core','cols'}, dimensions={0} | all-to-all | bytes 65536 | tf_op jit(solution)/shard_map/all_to_all | solution.py:306
  89.8 1.5 %last.1 = f32[8,2048]{1,0:T(8,128)} custom-call(f32[32,2,128]{2,1,0:T(2,128)S(1)} %all_to_all.16.gathered, f32[192,128]{1,0:T(8,128)S(1)} %get-tuple-element.23.mwin, f32[24,2304]{1,0:T(8,128)S(1)} %get-tuple-element.24.pre, f32[24,2304]{1,0:T(8,128)S(1)} %get-tuple-element.25.z_i, f32[24,2304]{1,0:T(8,128)S(1)} %get-tuple-element.26.wt, ...), custom_call_target="tpu_custom_call" | custom-call | tf_op jit(solution)/shard_map/last/pallas_call | solution.py:307
  (4 shorter events, 0.1 us)
Async XLA Ops:
  2.0 17.7 %copy-start.6 = (f32[400,128]{1,0:T(8,128)S(1)}, f32[400,128]{1,0:T(8,128)}, u32[]{:S(2)}) copy-start(f32[400,128]{1,0:T(8,128)} %get-tuple-element.21) | copy-start | bytes 614404
  2.0 24.6 %copy-start = (f32[8,2048]{1,0:T(8,128)S(1)}, f32[8,2048]{1,0:T(8,128)}, u32[]{:S(2)}) copy-start(f32[8,2048]{1,0:T(8,128)} %bf.1) | copy-start | bytes 196612
  2.0 24.6 %copy-start.1 = (f32[8,2048]{1,0:T(8,128)S(1)}, f32[8,2048]{1,0:T(8,128)}, u32[]{:S(2)}) copy-start(f32[8,2048]{1,0:T(8,128)} %rf.1) | copy-start | bytes 196612
  2.0 24.6 %copy-start.2 = (f32[8,2048]{1,0:T(8,128)S(1)}, f32[8,2048]{1,0:T(8,128)}, u32[]{:S(2)}) copy-start(f32[8,2048]{1,0:T(8,128)} %cf.1) | copy-start | bytes 196612
  2.1 24.6 %copy-start.3 = (f32[8,2048]{1,0:T(8,128)S(1)}, f32[8,2048]{1,0:T(8,128)}, u32[]{:S(2)}) copy-start(f32[8,2048]{1,0:T(8,128)} %lf.1) | copy-start | bytes 196612
  2.1 24.6 %copy-start.4 = (f32[8,2048]{1,0:T(8,128)S(1)}, f32[8,2048]{1,0:T(8,128)}, u32[]{:S(2)}) copy-start(f32[8,2048]{1,0:T(8,128)} %get-tuple-element.18.w) | copy-start | bytes 196612
  2.1 24.6 %copy-start.5 = (f32[32,128]{1,0:T(8,128)S(1)}, f32[32,128]{1,0:T(8,128)}, u32[]{:S(2)}) copy-start(f32[32,128]{1,0:T(8,128)} %get-tuple-element.19.mflat) | copy-start | bytes 49156
  2.1 24.6 %all-to-all-start = ((f32[8,72,128]{2,1,0:T(8,128)}), f32[8,72,128]{2,1,0:T(8,128)S(1)}, u32[]{:S(2)}, u32[]{:S(2)}) async-start(f32[8,72,128]{2,1,0:T(8,128)} %get-tuple-element.20), calls=%async_computation | async-start | bytes 589824 | tf_op jit(solution)/shard_map/all_to_all | solution.py:289
  19.7 3.3 %collective-permute-start = (f32[400,128]{1,0:T(8,128)S(1)}, f32[400,128]{1,0:T(8,128)S(1)}, u32[]{:S(2)}, u32[]{:S(2)}) collective-permute-start(f32[400,128]{1,0:T(8,128)S(1)} %copy-done.6), channel_id=1, source_target_pairs={{0,4},{4,0},{1,5},{5,1},{2,6},{6,2},{3,7},{7,3},{8,12},{12,8},{9,1... | collective-permute-start | bytes 614408 | tf_op jit(solution)/shard_map/ppermute | solution.py:288
  26.8 7.5 %collective-permute-start.1 = (f32[480,128]{1,0:T(8,128)S(1)}, f32[480,128]{1,0:T(8,128)S(1)}, u32[]{:S(2)}, u32[]{:S(2)}) collective-permute-start(f32[480,128]{1,0:T(8,128)S(1)} %chip.1), channel_id=1, source_target_pairs={{4,8},{8,4},{12,16},{16,12},{20,24},{24,20},{28,32},{32,28},{36,40... | collective-permute-start | bytes 737288 | tf_op jit(solution)/shard_map/ppermute | solution.py:297

commit v3 on v2

v3 whole, which is shorter than its diff:
```python
import functools

import jax
import jax.numpy as jnp
from jax import lax
from jax.experimental import pallas as pl
from jax.experimental.pallas import tpu as pltpu
from jax.sharding import Mesh
from jax.sharding import PartitionSpec as P

THETA = 1.05
DELTA = 0.95
OMEGA = 2.0 / 3.0
RHO0 = DELTA / THETA
RHO1 = 1.0 / (2.0 * THETA / DELTA - RHO0)
RHO2 = 1.0 / (2.0 * THETA / DELTA - RHO1)
LANES = 128
HALO = 4
WROWS = 24
ROWAX = ("x", "z", "core")
VMEM_LIMIT = 48 * 1024 * 1024
FIRST_LIMIT = 61 * 1024 * 1024


def call(kernel, outs, nin, name, space=pltpu.VMEM, scratch=(), limit=VMEM_LIMIT):
    return pl.pallas_call(
        kernel,
        out_shape=outs,
        in_specs=[pl.BlockSpec(memory_space=space)] * nin,
        out_specs=jax.tree.map(lambda _: pl.BlockSpec(memory_space=pltpu.VMEM), outs),
        scratch_shapes=scratch,
        compiler_params=pltpu.CompilerParams(vmem_limit_bytes=limit),
        name=name,
    )


def f32(*shape):
    return jax.ShapeDtypeStruct(shape, jnp.float32)


def weights(group, agg, w_ref):
    pairs = w_ref.shape[1] // 256
    per_row = 3 * pairs
    lane = lax.broadcasted_iota(jnp.int32, (8, LANES), 1)
    row = lax.broadcasted_iota(jnp.int32, (8, LANES), 0)
    for j in range(pairs):
        base = (row * pairs + j) * 256
        p1 = agg[pl.ds(3 * j + 1, 8, stride=per_row), :]
        p2 = agg[pl.ds(3 * j + 2, 8, stride=per_row), :]
        p1 = jnp.broadcast_to(p1[:, 0:1], (8, LANES)) - base
        p2 = jnp.broadcast_to(p2[:, 0:1], (8, LANES)) - base
        s0 = 1.0 / jnp.sqrt(p1.astype(jnp.float32) * float(group))
        s1 = 1.0 / jnp.sqrt((p2 - p1).astype(jnp.float32) * float(group))
        s2 = 1.0 / jnp.sqrt((256 - p2).astype(jnp.float32) * float(group))
        for half in range(2):
            at = lane + half * LANES
            value = jnp.where(at < p1, s0, jnp.where(at < p2, s1, s2))
            w_ref[:, (2 * j + half) * LANES : (2 * j + half + 1) * LANES] = value


def first_kernel(group, rhs, cr, cc, lk, agg, m, w_o, mflat, edges, b_v, r_v, c_v, l_v, agg_v, m_v, sems):
    n = w_o.shape[1]
    copies = []
    for i, (src, dst) in enumerate(((agg, agg_v), (m, m_v), (rhs, b_v), (cr, r_v), (cc, c_v), (lk, l_v))):
        for at in (slice(0, LANES), slice(n - LANES, n)):
            if i < 2:
                copy = pltpu.make_async_copy(src, dst, sems.at[len(copies)])
            else:
                copy = pltpu.make_async_copy(src.at[:, at], dst.at[:, at], sems.at[len(copies)])
            copies.append(copy)
            if i < 2:
                break
    for copy in copies:
        copy.start()
    for copy in copies:
        copy.wait()
    weights(group, agg_v, w_o)
    tiles = m.shape[1] // LANES
    for k in range(4):
        for t in range(tiles):
            mflat[k * tiles + t : k * tiles + t + 1, :] = m_v[k : k + 1, t * LANES : (t + 1) * LANES]
    refs = (b_v, l_v, r_v, c_v, w_o)
    mine = mflat[...]
    left = jnp.concatenate([x[:, 0:LANES] for x in refs] + [mine], axis=0)
    right = jnp.concatenate([x[:, n - LANES : n] for x in refs] + [mine], axis=0)
    me = lax.axis_index("cols")
    for c in range(edges.shape[0]):
        edges[c] = jnp.where(me > c, left, right)


def side_block(got, step):
    cols = lax.axis_size("cols")
    c = lax.axis_index("cols") + step
    ok = jnp.logical_and(c >= 0, c < cols)
    return jnp.where(ok, got[jnp.clip(c, 0, cols - 1)], 0.0)


def widened(left, own, right):
    return jnp.concatenate([left, own, right], axis=1)


def halves(left, x, right, i):
    return widened(left[8 * i : 8 * i + 8], x[...], right[8 * i : 8 * i + 8])


def operator(l, r, c, inside):
    west, north = pltpu.roll(r, 1, 1), pltpu.roll(c, 1, 0)
    diag = l + r + c + west + north
    inv = jnp.where(inside, 1.0 / jnp.where(inside, diag, 1.0), 0.0)
    return diag, inv, (r * inv, west * inv, c * inv, north * inv)


def rows_kernel(b, r, c, l, got, core_msg, chip_msg):
    lower = lax.axis_index("core") == 1
    left, right = side_block(got, -1), side_block(got, 1)
    bw, lw, rw, cw = [halves(left, x, right, i) for i, x in enumerate((b, l, r, c))]
    _, inv, coef = operator(lw, rw, cw, lw > 0.0)
    z0 = bw * inv
    z1 = z0 - scaled_apply(z0 * (1.0 / THETA), *coef)
    row = lax.broadcasted_iota(jnp.int32, bw.shape, 0)
    far = jnp.logical_or(row == 3, row == 4)
    fields = (jnp.where(far, z0, bw), jnp.where(far, z1, lw), rw, cw)
    up = jnp.concatenate([x[0:4] for x in fields], axis=0)
    down = jnp.concatenate([x[4:8] for x in fields], axis=0)
    core_msg[...] = jnp.where(lower, up, down)
    chip_msg[...] = jnp.where(lower, down, up)


def share_kernel(w, mflat, got, core_late, chip_late):
    lower = lax.axis_index("core") == 1
    left, right = side_block(got, -1), side_block(got, 1)
    ww = halves(left, w, right, 4)
    half = mflat.shape[0] // 2
    mats = (left[40:], mflat[...], right[40:])
    ncol = ww.shape[1] // LANES
    late_up = [ww[0:4, t * LANES : (t + 1) * LANES] for t in range(ncol)] + [x[:half] for x in mats]
    late_down = [ww[4:8, t * LANES : (t + 1) * LANES] for t in range(ncol)] + [x[half:] for x in mats]
    late_up, late_down = jnp.concatenate(late_up, axis=0), jnp.concatenate(late_down, axis=0)
    core_late[...] = jnp.where(lower, late_up, late_down)
    chip_late[...] = jnp.where(lower, late_down, late_up)


def shifted(v):
    n = v.shape[1]
    r = v.shape[0]
    return (pltpu.roll(v, n - 1, 1), pltpu.roll(v, 1, 1), pltpu.roll(v, r - 1, 0), pltpu.roll(v, 1, 0))


def scaled_apply(v, east, west, south, north):
    e, w, s, n = shifted(v)
    return v - east * e - west * w - south * s - north * n


def middle(b, r, c, l, w, got, s2, s1, pre_o, z_o, east_o, west_o, south_o, north_o, msg):
    upper = lax.axis_index("core") == 0
    left, right = side_block(got, -1), side_block(got, 1)
    pair, chip = s1[...], s2[...]
    above, below = jnp.where(upper, chip, pair), jnp.where(upper, pair, chip)
    pad = jnp.zeros((8 - HALO, above.shape[1]), jnp.float32)
    wins = []
    for i, x in enumerate((b, l, r, c)):
        at = slice(HALO * i, HALO * (i + 1))
        wins.append(jnp.concatenate([pad, above[at], halves(left, x, right, i), below[at], pad], axis=0))
    bw, lw, rw, cw = wins
    n = bw.shape[1]
    ncol = n // LANES - 2
    row = lax.broadcasted_iota(jnp.int32, bw.shape, 0)
    far = jnp.logical_or(row == 4, row == 19)
    inside = jnp.logical_and(lw > 0.0, jnp.logical_not(far))
    diag, inv, coef = operator(lw, rw, cw, inside)
    z = jnp.where(far, bw, bw * inv)
    d = z * (1.0 / THETA)
    x = d
    z = jnp.where(far, lw, z - scaled_apply(d, *coef))
    d = (RHO1 * RHO0) * d + (2.0 * RHO1 / DELTA) * z
    x = x + d
    z = z - scaled_apply(d, *coef)
    d = (RHO2 * RHO1) * d + (2.0 * RHO2 / DELTA) * z
    x = x + d
    z = z - scaled_apply(d, *coef)
    own = slice(8, 16)
    g = diag[own] * (z - OMEGA * scaled_apply(z, *coef))[own]
    part = jnp.zeros((8, LANES), jnp.float32)
    for t in range(ncol):
        part = part + w[:, t * LANES : (t + 1) * LANES] * g[:, (t + 1) * LANES : (t + 2) * LANES]
    pre_o[...] = x
    z_o[...] = z
    for ref, value in zip((east_o, west_o, south_o, north_o), coef):
        ref[...] = value
    total = jnp.sum(part, axis=1, keepdims=True)
    place = (lax.axis_index("z") * 2 + lax.axis_index("core")) * 4
    lane = lax.broadcasted_iota(jnp.int32, (8, LANES), 1)
    row = lax.broadcasted_iota(jnp.int32, (8, LANES), 0)
    spread = jnp.where(lane == lax.rem(place, LANES) + row // 2, total, 0.0)
    line = jnp.sum(spread, axis=0, keepdims=True)
    rows = lax.broadcasted_iota(jnp.int32, (msg.shape[1], LANES), 0)
    msg[...] = jnp.broadcast_to(jnp.where(rows == place // LANES, line, 0.0)[None], msg.shape)


def late_kernel(w, mflat, got, s1, s2, wt, mwin):
    upper = lax.axis_index("core") == 0
    left, right = side_block(got, -1), side_block(got, 1)
    pair, chip = s1[...], s2[...]
    above, below = jnp.where(upper, chip, pair), jnp.where(upper, pair, chip)
    ww = halves(left, w, right, 4)
    ncol = ww.shape[1] // LANES
    pad = jnp.zeros((8 - HALO, LANES), jnp.float32)
    for t in range(ncol):
        at = slice(HALO * t, HALO * (t + 1))
        s = slice(t * LANES, (t + 1) * LANES)
        wt[:, s] = jnp.concatenate([pad, above[at], ww[:, s], below[at], pad], axis=0)
    half = mflat.shape[0] // 2
    for i, mine in enumerate((left[40:], mflat[...], right[40:])):
        at = slice(HALO * ncol + half * i, HALO * ncol + half * (i + 1))
        mwin[4 * half * i : 4 * half * i + half, :] = above[at]
        mwin[4 * half * i + half : 4 * half * i + 3 * half, :] = mine
        mwin[4 * half * i + 3 * half : 4 * half * (i + 1), :] = below[at]


def last(xs, gathered, mwin, pre, z_i, wt, east, west, south, north, out):
    ncols = lax.axis_size("cols")
    tiles = mwin.shape[0] // 24
    mats = [[mwin[tiles * (8 * g + k) : tiles * (8 * g + k + 1), :] for k in range(8)] for g in range(3)]
    me = lax.axis_index("cols")
    blank = jnp.zeros((4, LANES), jnp.float32)

    def corrections(group, mats):
        v = []
        for x in range(xs):
            v.append(gathered[(2 * x) * ncols + group] + gathered[(2 * x + 1) * ncols + group])
        v = jnp.concatenate(v, axis=0)
        lines = [blank]
        for m in mats:
            p = jnp.sum(m * v, axis=0, keepdims=True)
            lines += [p, p]
        lines.append(blank)
        return jnp.sum(jnp.concatenate(lines, axis=0), axis=1, keepdims=True)

    cl = corrections(jnp.maximum(me - 1, 0), mats[0])
    co = corrections(me, mats[1])
    cn = corrections(jnp.minimum(me + 1, ncols - 1), mats[2])
    w = wt[...]
    n = w.shape[1]
    lane = lax.broadcasted_iota(jnp.int32, (1, n), 1)
    lifted = w * jnp.where(lane < LANES, cl, jnp.where(lane >= n - LANES, cn, co))
    op = functools.partial(scaled_apply, east=east[...], west=west[...], south=south[...], north=north[...])
    e = lifted - OMEGA * op(lifted)
    x = pre[...] + e
    z = z_i[...] - op(e)
    d = z * (1.0 / THETA)
    x = x + d
    z = z - op(d)
    d = (RHO1 * RHO0) * d + (2.0 * RHO1 / DELTA) * z
    x = x + d
    z = z - op(d)
    d = (RHO2 * RHO1) * d + (2.0 * RHO2 / DELTA) * z
    x = x + d
    out[...] = x[8:16, LANES : n - LANES]


def local(sizes, rhs, cond_row, cond_col, leak, agg_members, coarse_inverse):
    xs, zs, cores, cols = sizes
    width = rhs.shape[1]
    wide = width + 2 * LANES
    m = coarse_inverse[0]
    tiles = m.shape[1] // LANES
    group = agg_members.shape[2] // 4
    agg = agg_members[0, 0]
    block = f32(8, width)
    w, mflat, edges = call(
        functools.partial(first_kernel, group),
        [block, f32(4 * tiles, LANES), f32(cols, 40 + 4 * tiles, LANES)],
        6,
        "first",
        space=pltpu.HBM,
        limit=FIRST_LIMIT,
        scratch=[pltpu.VMEM((8, width), jnp.float32)] * 4
        + [
            pltpu.VMEM(agg.shape, jnp.int32),
            pltpu.VMEM(m.shape, jnp.float32),
            pltpu.SemaphoreType.DMA((10,)),
        ],
    )(rhs, cond_row, cond_col, leak, agg, m)
    b, r, c, l = rhs, cond_row, cond_col, leak
    got = lax.all_to_all(edges, "cols", 0, 0, tiled=True)
    message = f32(4 * HALO, wide)
    late = f32(HALO * wide // LANES + 6 * tiles, LANES)
    devices = xs * zs * cores
    swap = []
    for i in range(1, devices - 1, 2):
        swap += [(i, i + 1), (i + 1, i)]
    core_msg, chip_msg = call(rows_kernel, [message, message], 5, "rows")(b, r, c, l, got)
    s2 = lax.ppermute(chip_msg, ROWAX, swap)
    s1 = lax.ppermute(core_msg, "core", [(0, 1), (1, 0)])
    per_x = max(1, zs * cores * 4 // LANES)
    win = f32(WROWS, wide)
    pre, z, east, west, south, north, msg = call(middle, [win] * 6 + [f32(zs, per_x, LANES)], 8, "middle")(
        b, r, c, l, w, got, s2, s1
    )
    spread = lax.all_to_all(msg, "z", 0, 0, tiled=True)
    core_late, chip_late = call(share_kernel, [late, late], 3, "share")(w, mflat, got)
    s2_late = lax.ppermute(chip_late, ROWAX, swap)
    s1_late = lax.ppermute(core_late, "core", [(0, 1), (1, 0)])
    wt, mwin = call(late_kernel, [win, f32(24 * tiles, LANES)], 5, "late")(w, mflat, got, s1_late, s2_late)
    line = jnp.sum(spread, axis=0)
    second = jnp.broadcast_to(line[None], (xs * cores * cols, per_x, LANES))
    gathered = lax.all_to_all(second, ("x", "core", "cols"), 0, 0, tiled=True)
    return call(functools.partial(last, xs), block, 9, "last")(
        gathered, mwin, pre, z, wt, east, west, south, north
    )


def solution(mesh):
    rows, cols = mesh.shape["rows"], mesh.shape["cols"]
    cores = 2
    xs = 4 if rows == 256 else 2
    zs = rows // (xs * cores)
    fine = Mesh(mesh.devices.reshape(xs, zs, cores, cols), ("x", "z", "core", "cols"))
    spec = P(ROWAX, "cols")
    in_specs = (spec, spec, spec, spec, P(ROWAX, "cols", None, None), P("cols", ROWAX, None))
    return jax.shard_map(
        functools.partial(local, (xs, zs, cores, cols)),
        mesh=fine,
        in_specs=in_specs,
        out_specs=spec,
        check_vma=False,
    )
```

time: 91.6 us -> 90.6 us (0.989)
  blocking collectives: 54.4 us -> 10.1 us
  starting transfers between devices: 21.6 us -> 51.2 us
  waiting for transfers between devices: 10.5 us -> 22.7 us
    all_to_all x2 -> x1, blocking collectives: 54.4 us -> 10.1 us  [local(): got = lax.all_to_all(edges, 'cols', 0, 0, tiled=True)]
    all_to_all x1 -> x2, waiting for transfers between devices: 3.57 us -> 21.7 us  [the longest x1 14.6 us: local(): spread = lax.all_to_all(msg, 'z', 0, 0, tiled=True)]
    all_to_all x1 -> x2, starting transfers between devices: 17.6 us -> 27.7 us  [the longest x1 19.3 us: local(): spread = lax.all_to_all(msg, 'z', 0, 0, tiled=True)]
    ppermute x1, starting transfers between devices: 2 us -> 10.6 us  [local(): s1 = lax.ppermute(core_msg, 'core', [(0, 1), (1, 0)])]
    ppermute x0 -> x2, starting transfers between devices: none -> 7.38 us  [the longest x1 4.06 us: local(): s1_late = lax.ppermute(core_late, 'core', [(0, 1), (1, 0)])]
    ppermute x1, waiting for transfers between devices: 5.59 us -> 0.01 us  [local(): s2 = lax.ppermute(chip_msg, ROWAX, swap)]
    ppermute x1, starting transfers between devices: 1.92 us -> 5.54 us  [local(): s2 = lax.ppermute(chip_msg, ROWAX, swap)]
    pallas_call x2 -> x4, Pallas kernels: 1.12 us -> 1.96 us  [the longest x1 1.69 us: local(): call(middle, [win] * 6 + [f32(zs, per_x, LANES)], 8, 'middle')]
  transfers between devices with their start and end apart: 3 -> 6, of which waited for: 3 -> 3; matrix products, arithmetic and copies ran while one was open for 0% -> 1% of each run, Pallas kernels for 0% -> 0%
where the time goes in v3:
time: 90.6 us; the launch traced here: 90.1 us
  starting transfers between devices  51.2 us (57%)
  waiting for transfers between devices  22.7 us (25%)
  blocking collectives  10.1 us (11%)
  Pallas kernels  5.19 us (6%)
    all_to_all x1, starting transfers between devices, local(): spread = lax.all_to_all(msg, 'z', 0, 0, tiled=True)  19.3 us
    all_to_all x1, waiting for transfers between devices, local(): spread = lax.all_to_all(msg, 'z', 0, 0, tiled=True)  14.6 us
    ppermute x1, starting transfers between devices, local(): s1 = lax.ppermute(core_msg, 'core', [(0, 1), (1, 0)])  10.6 us
    all_to_all x1, blocking collectives, local(): got = lax.all_to_all(edges, 'cols', 0, 0, tiled=True)  10.1 us
    all_to_all x1, starting transfers between devices, local(): gathered = lax.all_to_all(second, ('x', 'core', 'cols'), 0, 0, tiled=True)  8.35 us
    all_to_all x1, waiting for transfers between devices, local(): gathered = lax.all_to_all(second, ('x', 'core', 'cols'), 0, 0, tiled=True)  7.16 us
    ppermute x1, starting transfers between devices, local(): s2 = lax.ppermute(chip_msg, ROWAX, swap)  5.54 us
    ppermute x1, starting transfers between devices, local(): s1_late = lax.ppermute(core_late, 'core', [(0, 1), (1, 0)])  4.06 us
  transfers between devices with their start and end apart: 6, of which 3 were waited for; matrix products, arithmetic and copies ran while one was open for 1% of the time, Pallas kernels for 0%

profile of v3, /device:TPU:1, one launch (start us, length us, event | category | flops | bytes accessed | tf_op | source)
XLA Modules:
  0.0 90.1 jit_solution(3760427877547244380)
XLA Ops:
  0.0 1.8 %first.1 = (f32[8,2048]{1,0:T(8,128)}, f32[32,128]{1,0:T(8,128)}, f32[4,72,128]{2,1,0:T(8,128)}) custom-call(f32[8,2048]{1,0:T(8,128)} %b.3, f32[8,2048]{1,0:T(8,128)} %r.3, f32[8,2048]{1,0:T(8,128)} %c.3, f32[8,2048]{1,0:T(8,128)} %l.3, s32[192,128]{1,0:T(8,128)} %bitcast.2, f32[4,1024]{1,0:T(4,128)} %bitcast.3), custom_call_target="tpu_custom_call" | custom-call | tf_op jit(solution)/shard_map/first/pallas_call | solution.py:270
  1.8 0.0 copy-start
  1.8 0.0 copy-start.1
  1.8 0.0 copy-start.2
  1.8 0.0 copy-start.3
  1.8 10.1 %all_to_all.15.got = f32[4,72,128]{2,1,0:T(8,128)S(1)} all-to-all(f32[4,72,128]{2,1,0:T(8,128)} %get-tuple-element.22), channel_id=1, replica_groups=mesh['x'=4,'z'=32,'core'=2,'cols'=4] {'cols'}, dimensions={0} | all-to-all | bytes 294912 | tf_op jit(solution)/shard_map/all_to_all | solution.py:285
  11.9 0.0 copy-done
  11.9 0.0 copy-start.4
  11.9 0.2 rows.1
  12.2 5.5 %collective-permute-start = (f32[16,2304]{1,0:T(8,128)S(1)}, f32[16,2304]{1,0:T(8,128)S(1)}, u32[]{:S(2)}, u32[]{:S(2)}) collective-permute-start(f32[16,2304]{1,0:T(8,128)S(1)} %get-tuple-element.23), channel_id=1, source_target_pairs={{4,8},{8,4},{12,16},{16,12},{20,24},{24,20},{28,32},{32,28},{36,40... | collective-permute-start | bytes 442376 | tf_op jit(solution)/shard_map/ppermute | solution.py:293
  17.7 10.6 %collective-permute-start.1 = (f32[16,2304]{1,0:T(8,128)S(1)}, f32[16,2304]{1,0:T(8,128)S(1)}, u32[]{:S(2)}, u32[]{:S(2)}) collective-permute-start(f32[16,2304]{1,0:T(8,128)S(1)} %get-tuple-element.24), channel_id=1, source_target_pairs={{0,4},{4,0},{1,5},{5,1},{2,6},{6,2},{3,7},{7,3},{8,12},{12,8},{9,1... | collective-permute-start | bytes 442376 | tf_op jit(solution)/shard_map/ppermute | solution.py:294
  28.3 0.0 collective-permute-done.s2
  28.4 1.0 %collective-permute-done.1.s1 = f32[16,2304]{1,0:T(8,128)S(1)} collective-permute-done((f32[16,2304]{1,0:T(8,128)S(1)}, f32[16,2304]{1,0:T(8,128)S(1)}, u32[]{:S(2)}, u32[]{:S(2)}) %collective-permute-start.1) | collective-permute-done | bytes 147488 | tf_op jit(solution)/shard_map/ppermute | solution.py:294
  29.3 1.7 %middle.1 = (f32[24,2304]{1,0:T(8,128)S(1)}, f32[24,2304]{1,0:T(8,128)S(1)}, f32[24,2304]{1,0:T(8,128)S(1)}, f32[24,2304]{1,0:T(8,128)S(1)}, f32[24,2304]{1,0:T(...) custom-call(f32[8,2048]{1,0:T(8,128)S(1)} %copy-done, f32[8,2048]{1,0:T(8,128)S(1)} %copy-done.1, ...), custom_call_target="tpu_custom_call" | custom-call | tf_op jit(solution)/shard_map/middle/pallas_call | solution.py:297
  31.0 19.3 %all-to-all-start.1 = ((f32[32,2,128]{2,1,0:T(2,128)}), f32[32,2,128]{2,1,0:T(2,128)S(1)}, u32[]{:S(2)}, u32[]{:S(2)}) async-start(f32[32,2,128]{2,1,0:T(2,128)} %get-tuple-element.25), calls=%async_computation.1 | async-start | bytes 65536 | tf_op jit(solution)/shard_map/all_to_all | solution.py:300
  50.4 4.1 %collective-permute-start.2 = (f32[120,128]{1,0:T(8,128)S(1)}, f32[120,128]{1,0:T(8,128)S(1)}, u32[]{:S(2)}, u32[]{:S(2)}) collective-permute-start(f32[120,128]{1,0:T(8,128)S(1)} %get-tuple-element.27), channel_id=1, source_target_pairs={{0,4},{4,0},{1,5},{5,1},{2,6},{6,2},{3,7},{7,3},{8,12},{12,8},{9,1... | collective-permute-start | bytes 184328 | tf_op jit(solution)/shard_map/ppermute | solution.py:303
  54.5 3.3 %collective-permute-start.3 = (f32[120,128]{1,0:T(8,128)S(1)}, f32[120,128]{1,0:T(8,128)S(1)}, u32[]{:S(2)}, u32[]{:S(2)}) collective-permute-start(f32[120,128]{1,0:T(8,128)S(1)} %get-tuple-element.28), channel_id=1, source_target_pairs={{4,8},{8,4},{12,16},{16,12},{20,24},{24,20},{28,32},{32,28},{36,40... | collective-permute-start | bytes 184328 | tf_op jit(solution)/shard_map/ppermute | solution.py:302
  57.8 14.6 %all-to-all-done.1 = f32[32,2,128]{2,1,0:T(2,128)S(1)} async-done(((f32[32,2,128]{2,1,0:T(2,128)}), f32[32,2,128]{2,1,0:T(2,128)S(1)}, u32[]{:S(2)}, u32[]{:S(2)}) %all-to-all-start.1) | async-done | bytes 32800 | tf_op jit(solution)/shard_map/all_to_all | solution.py:300
  72.4 0.6 broadcast_in_dim.2
  73.0 8.4 %all-to-all-start.2 = ((f32[32,2,128]{2,1,0:T(2,128)}), f32[32,2,128]{2,1,0:T(2,128)S(1)}, u32[]{:S(2)}, u32[]{:S(2)}) async-start(f32[32,2,128]{2,1,0:T(2,128)} %broadcast_in_dim.2), calls=%async_computation.2 | async-start | bytes 65536 | tf_op jit(solution)/shard_map/all_to_all | solution.py:307
  81.4 0.0 collective-permute-done.2.s1
  81.4 0.0 collective-permute-done.3.s2
  81.5 7.2 %all-to-all-done.2.gathered = f32[32,2,128]{2,1,0:T(2,128)S(1)} async-done(((f32[32,2,128]{2,1,0:T(2,128)}), f32[32,2,128]{2,1,0:T(2,128)S(1)}, u32[]{:S(2)}, u32[]{:S(2)}) %all-to-all-start.2) | async-done | bytes 32800 | tf_op jit(solution)/shard_map/all_to_all | solution.py:307
  88.6 1.5 %last.1 = f32[8,2048]{1,0:T(8,128)} custom-call(f32[32,2,128]{2,1,0:T(2,128)S(1)} %all-to-all-done.2.gathered, f32[192,128]{1,0:T(8,128)S(1)} %get-tuple-element.29.mwin, f32[24,2304]{1,0:T(8,128)S(1)} %get-tuple-element.30.pre, f32[24,2304]{1,0:T(8,128)S(1)} %get-tuple-element.31.z_i, f32[24,2304]{1,0:T(8,128)S(1)} %get-tuple-element.32.wt, ...), custom_call_target="tpu_custom_call" | custom-call | tf_op jit(solution)/shard_map/last/pallas_call | solution.py:308
  (9 shorter events, 0.1 us)
Async XLA Ops:
  1.8 10.1 %copy-start = (f32[8,2048]{1,0:T(8,128)S(1)}, f32[8,2048]{1,0:T(8,128)}, u32[]{:S(2)}) copy-start(f32[8,2048]{1,0:T(8,128)} %b.3) | copy-start | bytes 196612
  1.8 10.1 %copy-start.1 = (f32[8,2048]{1,0:T(8,128)S(1)}, f32[8,2048]{1,0:T(8,128)}, u32[]{:S(2)}) copy-start(f32[8,2048]{1,0:T(8,128)} %r.3) | copy-start | bytes 196612
  1.8 10.1 %copy-start.2 = (f32[8,2048]{1,0:T(8,128)S(1)}, f32[8,2048]{1,0:T(8,128)}, u32[]{:S(2)}) copy-start(f32[8,2048]{1,0:T(8,128)} %c.3) | copy-start | bytes 196612
  1.8 10.1 %copy-start.3 = (f32[8,2048]{1,0:T(8,128)S(1)}, f32[8,2048]{1,0:T(8,128)}, u32[]{:S(2)}) copy-start(f32[8,2048]{1,0:T(8,128)} %l.3) | copy-start | bytes 196612
  11.9 17.4 %copy-start.4 = (f32[8,2048]{1,0:T(8,128)S(1)}, f32[8,2048]{1,0:T(8,128)}, u32[]{:S(2)}) copy-start(f32[8,2048]{1,0:T(8,128)} %get-tuple-element.21.w) | copy-start | bytes 196612
  12.2 16.2 %collective-permute-start = (f32[16,2304]{1,0:T(8,128)S(1)}, f32[16,2304]{1,0:T(8,128)S(1)}, u32[]{:S(2)}, u32[]{:S(2)}) collective-permute-start(f32[16,2304]{1,0:T(8,128)S(1)} %get-tuple-element.23), channel_id=1, source_target_pairs={{4,8},{8,4},{12,16},{16,12},{20,24},{24,20},{28,32},{32,28},{36,40... | collective-permute-start | bytes 442376 | tf_op jit(solution)/shard_map/ppermute | solution.py:293
  17.7 11.6 %collective-permute-start.1 = (f32[16,2304]{1,0:T(8,128)S(1)}, f32[16,2304]{1,0:T(8,128)S(1)}, u32[]{:S(2)}, u32[]{:S(2)}) collective-permute-start(f32[16,2304]{1,0:T(8,128)S(1)} %get-tuple-element.24), channel_id=1, source_target_pairs={{0,4},{4,0},{1,5},{5,1},{2,6},{6,2},{3,7},{7,3},{8,12},{12,8},{9,1... | collective-permute-start | bytes 442376 | tf_op jit(solution)/shard_map/ppermute | solution.py:294
  31.0 19.3 %copy-start.5 = (f32[32,128]{1,0:T(8,128)S(1)}, f32[32,128]{1,0:T(8,128)}, u32[]{:S(2)}) copy-start(f32[32,128]{1,0:T(8,128)} %get-tuple-element.26.mflat) | copy-start | bytes 49156
  31.0 41.3 %all-to-all-start.1 = ((f32[32,2,128]{2,1,0:T(2,128)}), f32[32,2,128]{2,1,0:T(2,128)S(1)}, u32[]{:S(2)}, u32[]{:S(2)}) async-start(f32[32,2,128]{2,1,0:T(2,128)} %get-tuple-element.25), calls=%async_computation.1 | async-start | bytes 65536 | tf_op jit(solution)/shard_map/all_to_all | solution.py:300
  50.4 31.0 %collective-permute-start.2 = (f32[120,128]{1,0:T(8,128)S(1)}, f32[120,128]{1,0:T(8,128)S(1)}, u32[]{:S(2)}, u32[]{:S(2)}) collective-permute-start(f32[120,128]{1,0:T(8,128)S(1)} %get-tuple-element.27), channel_id=1, source_target_pairs={{0,4},{4,0},{1,5},{5,1},{2,6},{6,2},{3,7},{7,3},{8,12},{12,8},{9,1... | collective-permute-start | bytes 184328 | tf_op jit(solution)/shard_map/ppermute | solution.py:303
  54.5 26.9 %collective-permute-start.3 = (f32[120,128]{1,0:T(8,128)S(1)}, f32[120,128]{1,0:T(8,128)S(1)}, u32[]{:S(2)}, u32[]{:S(2)}) collective-permute-start(f32[120,128]{1,0:T(8,128)S(1)} %get-tuple-element.28), channel_id=1, source_target_pairs={{4,8},{8,4},{12,16},{16,12},{20,24},{24,20},{28,32},{32,28},{36,40... | collective-permute-start | bytes 184328 | tf_op jit(solution)/shard_map/ppermute | solution.py:302
  73.0 15.6 %all-to-all-start.2 = ((f32[32,2,128]{2,1,0:T(2,128)}), f32[32,2,128]{2,1,0:T(2,128)S(1)}, u32[]{:S(2)}, u32[]{:S(2)}) async-start(f32[32,2,128]{2,1,0:T(2,128)} %broadcast_in_dim.2), calls=%async_computation.2 | async-start | bytes 65536 | tf_op jit(solution)/shard_map/all_to_all | solution.py:307

commit v4 on v3

--- a/solution.py
+++ b/solution.py
@@ -16,7 +16,7 @@
 RHO2 = 1.0 / (2.0 * THETA / DELTA - RHO1)
 LANES = 128
 HALO = 4
-WROWS = 24
+WROWS = 16
 ROWAX = ("x", "z", "core")
 VMEM_LIMIT = 48 * 1024 * 1024
 FIRST_LIMIT = 61 * 1024 * 1024
@@ -58,8 +58,15 @@
             w_ref[:, (2 * j + half) * LANES : (2 * j + half + 1) * LANES] = value
 
 
-def first_kernel(group, rhs, cr, cc, lk, agg, m, w_o, mflat, edges, b_v, r_v, c_v, l_v, agg_v, m_v, sems):
-    n = w_o.shape[1]
+def flatten(m, mflat):
+    tiles = m.shape[1] // LANES
+    for k in range(4):
+        for t in range(tiles):
+            mflat[k * tiles + t : k * tiles + t + 1, :] = m[k : k + 1, t * LANES : (t + 1) * LANES]
+
+
+def first_kernel(group, rhs, cr, cc, lk, agg, m, edges, b_v, r_v, c_v, l_v, agg_v, m_v, w_v, mflat, sems):
+    n = w_v.shape[1]
     copies = []
     for i, (src, dst) in enumerate(((agg, agg_v), (m, m_v), (rhs, b_v), (cr, r_v), (cc, c_v), (lk, l_v))):
         for at in (slice(0, LANES), slice(n - LANES, n)):
@@ -74,12 +81,9 @@
         copy.start()
     for copy in copies:
         copy.wait()
-    weights(group, agg_v, w_o)
-    tiles = m.shape[1] // LANES
-    for k in range(4):
-        for t in range(tiles):
-            mflat[k * tiles + t : k * tiles + t + 1, :] = m_v[k : k + 1, t * LANES : (t + 1) * LANES]
-    refs = (b_v, l_v, r_v, c_v, w_o)
+    weights(group, agg_v, w_v)
+    flatten(m_v, mflat)
+    refs = (b_v, l_v, r_v, c_v, w_v)
     mine = mflat[...]
     left = jnp.concatenate([x[:, 0:LANES] for x in refs] + [mine], axis=0)
     right = jnp.concatenate([x[:, n - LANES : n] for x in refs] + [mine], axis=0)
@@ -110,9 +114,7 @@
     return diag, inv, (r * inv, west * inv, c * inv, north * inv)
 
 
-def rows_kernel(b, r, c, l, got, core_msg, chip_msg):
-    lower = lax.axis_index("core") == 1
-    left, right = side_block(got, -1), side_block(got, 1)
+def row_messages(b, r, c, l, left, right):
     bw, lw, rw, cw = [halves(left, x, right, i) for i, x in enumerate((b, l, r, c))]
     _, inv, coef = operator(lw, rw, cw, lw > 0.0)
     z0 = bw * inv
@@ -122,21 +124,28 @@
     fields = (jnp.where(far, z0, bw), jnp.where(far, z1, lw), rw, cw)
     up = jnp.concatenate([x[0:4] for x in fields], axis=0)
     down = jnp.concatenate([x[4:8] for x in fields], axis=0)
-    core_msg[...] = jnp.where(lower, up, down)
-    chip_msg[...] = jnp.where(lower, down, up)
-
-
-def share_kernel(w, mflat, got, core_late, chip_late):
+    return up, down
+
+
+def rows_kernel(group, b, r, c, l, agg, m, got, chip_msg, core_msg, chip_late, w, mflat):
+    weights(group, agg, w)
+    flatten(m, mflat)
     lower = lax.axis_index("core") == 1
     left, right = side_block(got, -1), side_block(got, 1)
+    up, down = row_messages(b, r, c, l, left, right)
+    chip_msg[...] = jnp.where(lower, down, up)
+    message = jnp.where(lower, up, down)
     ww = halves(left, w, right, 4)
     half = mflat.shape[0] // 2
     mats = (left[40:], mflat[...], right[40:])
     ncol = ww.shape[1] // LANES
+    rows = 4 * HALO
+    for t in range(ncol):
+        core_msg[rows * t : rows * (t + 1), :] = message[:, t * LANES : (t + 1) * LANES]
     late_up = [ww[0:4, t * LANES : (t + 1) * LANES] for t in range(ncol)] + [x[:half] for x in mats]
     late_down = [ww[4:8, t * LANES : (t + 1) * LANES] for t in range(ncol)] + [x[half:] for x in mats]
     late_up, late_down = jnp.concatenate(late_up, axis=0), jnp.concatenate(late_down, axis=0)
-    core_late[...] = jnp.where(lower, late_up, late_down)
+    core_msg[rows * ncol :, :] = jnp.where(lower, late_up, late_down)
     chip_late[...] = jnp.where(lower, late_down, late_up)
 
 
@@ -154,18 +163,19 @@
 def middle(b, r, c, l, w, got, s2, s1, pre_o, z_o, east_o, west_o, south_o, north_o, msg):
     upper = lax.axis_index("core") == 0
     left, right = side_block(got, -1), side_block(got, 1)
-    pair, chip = s1[...], s2[...]
+    chip = s2[...]
+    rows = 4 * HALO
+    pair = jnp.concatenate([s1[rows * t : rows * (t + 1), :] for t in range(chip.shape[1] // LANES)], axis=1)
     above, below = jnp.where(upper, chip, pair), jnp.where(upper, pair, chip)
-    pad = jnp.zeros((8 - HALO, above.shape[1]), jnp.float32)
     wins = []
     for i, x in enumerate((b, l, r, c)):
         at = slice(HALO * i, HALO * (i + 1))
-        wins.append(jnp.concatenate([pad, above[at], halves(left, x, right, i), below[at], pad], axis=0))
+        wins.append(jnp.concatenate([halves(left, x, right, i), below[at], above[at]], axis=0))
     bw, lw, rw, cw = wins
     n = bw.shape[1]
     ncol = n // LANES - 2
     row = lax.broadcasted_iota(jnp.int32, bw.shape, 0)
-    far = jnp.logical_or(row == 4, row == 19)
+    far = jnp.logical_or(row == 11, row == 12)
     inside = jnp.logical_and(lw > 0.0, jnp.logical_not(far))
     diag, inv, coef = operator(lw, rw, cw, inside)
     z = jnp.where(far, bw, bw * inv)
@@ -178,7 +188,7 @@
     d = (RHO2 * RHO1) * d + (2.0 * RHO2 / DELTA) * z
     x = x + d
     z = z - scaled_apply(d, *coef)
-    own = slice(8, 16)
+    own = slice(0, 8)
     g = diag[own] * (z - OMEGA * scaled_apply(z, *coef))[own]
     part = jnp.zeros((8, LANES), jnp.float32)
     for t in range(ncol):
@@ -200,15 +210,14 @@
 def late_kernel(w, mflat, got, s1, s2, wt, mwin):
     upper = lax.axis_index("core") == 0
     left, right = side_block(got, -1), side_block(got, 1)
-    pair, chip = s1[...], s2[...]
+    pair, chip = s1[s1.shape[0] - s2.shape[0] :, :], s2[...]
     above, below = jnp.where(upper, chip, pair), jnp.where(upper, pair, chip)
     ww = halves(left, w, right, 4)
     ncol = ww.shape[1] // LANES
-    pad = jnp.zeros((8 - HALO, LANES), jnp.float32)
     for t in range(ncol):
         at = slice(HALO * t, HALO * (t + 1))
         s = slice(t * LANES, (t + 1) * LANES)
-        wt[:, s] = jnp.concatenate([pad, above[at], ww[:, s], below[at], pad], axis=0)
+        wt[:, s] = jnp.concatenate([ww[:, s], below[at], above[at]], axis=0)
     half = mflat.shape[0] // 2
     for i, mine in enumerate((left[40:], mflat[...], right[40:])):
         at = slice(HALO * ncol + half * i, HALO * ncol + half * (i + 1))
@@ -222,18 +231,16 @@
     tiles = mwin.shape[0] // 24
     mats = [[mwin[tiles * (8 * g + k) : tiles * (8 * g + k + 1), :] for k in range(8)] for g in range(3)]
     me = lax.axis_index("cols")
-    blank = jnp.zeros((4, LANES), jnp.float32)
 
     def corrections(group, mats):
         v = []
         for x in range(xs):
             v.append(gathered[(2 * x) * ncols + group] + gathered[(2 * x + 1) * ncols + group])
         v = jnp.concatenate(v, axis=0)
-        lines = [blank]
-        for m in mats:
+        lines = []
+        for m in mats[2:] + mats[:2]:
             p = jnp.sum(m * v, axis=0, keepdims=True)
             lines += [p, p]
-        lines.append(blank)
         return jnp.sum(jnp.concatenate(lines, axis=0), axis=1, keepdims=True)
 
     cl = corrections(jnp.maximum(me - 1, 0), mats[0])
@@ -255,7 +262,7 @@
     z = z - op(d)
     d = (RHO2 * RHO1) * d + (2.0 * RHO2 / DELTA) * z
     x = x + d
-    out[...] = x[8:16, LANES : n - LANES]
+    out[...] = x[0:8, LANES : n - LANES]
 
 
 def local(sizes, rhs, cond_row, cond_col, leak, agg_members, coarse_inverse):
@@ -267,9 +274,9 @@
     group = agg_members.shape[2] // 4
     agg = agg_members[0, 0]
     block = f32(8, width)
-    w, mflat, edges = call(
+    edges = call(
         functools.partial(first_kernel, group),
-        [block, f32(4 * tiles, LANES), f32(cols, 40 + 4 * tiles, LANES)],
+        f32(cols, 40 + 4 * tiles, LANES),
         6,
         "first",
         space=pltpu.HBM,
@@ -278,18 +285,24 @@
         + [
             pltpu.VMEM(agg.shape, jnp.int32),
             pltpu.VMEM(m.shape, jnp.float32),
+            pltpu.VMEM((8, width), jnp.float32),
+            pltpu.VMEM((4 * tiles, LANES), jnp.float32),
             pltpu.SemaphoreType.DMA((10,)),
         ],
     )(rhs, cond_row, cond_col, leak, agg, m)
     b, r, c, l = rhs, cond_row, cond_col, leak
     got = lax.all_to_all(edges, "cols", 0, 0, tiled=True)
-    message = f32(4 * HALO, wide)
-    late = f32(HALO * wide // LANES + 6 * tiles, LANES)
     devices = xs * zs * cores
     swap = []
     for i in range(1, devices - 1, 2):
         swap += [(i, i + 1), (i + 1, i)]
-    core_msg, chip_msg = call(rows_kernel, [message, message], 5, "rows")(b, r, c, l, got)
+    late = HALO * wide // LANES + 6 * tiles
+    chip_msg, core_msg, chip_late, w, mflat = call(
+        functools.partial(rows_kernel, group),
+        [f32(4 * HALO, wide), f32(4 * HALO * wide // LANES + late, LANES), f32(late, LANES), block, f32(4 * tiles, LANES)],
+        7,
+        "rows",
+    )(b, r, c, l, agg, m, got)
     s2 = lax.ppermute(chip_msg, ROWAX, swap)
     s1 = lax.ppermute(core_msg, "core", [(0, 1), (1, 0)])
     per_x = max(1, zs * cores * 4 // LANES)
@@ -298,10 +311,8 @@
         b, r, c, l, w, got, s2, s1
     )
     spread = lax.all_to_all(msg, "z", 0, 0, tiled=True)
-    core_late, chip_late = call(share_kernel, [late, late], 3, "share")(w, mflat, got)
     s2_late = lax.ppermute(chip_late, ROWAX, swap)
-    s1_late = lax.ppermute(core_late, "core", [(0, 1), (1, 0)])
-    wt, mwin = call(late_kernel, [win, f32(24 * tiles, LANES)], 5, "late")(w, mflat, got, s1_late, s2_late)
+    wt, mwin = call(late_kernel, [win, f32(24 * tiles, LANES)], 5, "late")(w, mflat, got, s1, s2_late)
     line = jnp.sum(spread, axis=0)
     second = jnp.broadcast_to(line[None], (xs * cores * cols, per_x, LANES))
     gathered = lax.all_to_all(second, ("x", "core", "cols"), 0, 0, tiled=True)

time: 90.6 us -> 91.7 us (1.012)
  waiting for transfers between devices: 22.7 us -> 29.2 us
  starting transfers between devices: 51.2 us -> 46.6 us
    ppermute x1, starting transfers between devices: 10.6 us -> 15.5 us  [local(): s1 = lax.ppermute(core_msg, 'core', [(0, 1), (1, 0)])]
    ppermute x1, waiting for transfers between devices: 0.01 us -> 4.53 us  [local(): s2 = lax.ppermute(chip_msg, ROWAX, swap)]
    ppermute x1 -> x0, starting transfers between devices: 4.06 us -> none  [local(): s1_late = lax.ppermute(core_late, 'core', [(0, 1), (1, 0)])]
    ppermute x1, starting transfers between devices: 5.54 us -> 1.92 us  [local(): s2 = lax.ppermute(chip_msg, ROWAX, swap)]
    all_to_all x1, waiting for transfers between devices: 14.6 us -> 17.5 us  [local(): spread = lax.all_to_all(msg, 'z', 0, 0, tiled=True)]
    all_to_all x1, starting transfers between devices: 19.3 us -> 17.3 us  [local(): spread = lax.all_to_all(msg, 'z', 0, 0, tiled=True)]
    ppermute x1, starting transfers between devices: 3.32 us -> 4.51 us  [local(): s2_late = lax.ppermute(chip_late, ROWAX, swap)]
    ppermute x1, waiting for transfers between devices: 0.97 us -> 0.01 us  [local(): s1 = lax.ppermute(core_msg, 'core', [(0, 1), (1, 0)])]
  transfers between devices with their start and end apart: 6 -> 5, of which waited for: 3 -> 3; matrix products, arithmetic and copies ran while one was open for 1% -> 1% of each run, Pallas kernels for 0% -> 0%
where the time goes in v4:
time: 91.7 us; the launch traced here: 91.3 us
  starting transfers between devices  46.6 us (51%)
  waiting for transfers between devices  29.2 us (32%)
  blocking collectives  10.1 us (11%)
  Pallas kernels  4.59 us (5%)
    all_to_all x1, waiting for transfers between devices, local(): spread = lax.all_to_all(msg, 'z', 0, 0, tiled=True)  17.5 us
    all_to_all x1, starting transfers between devices, local(): spread = lax.all_to_all(msg, 'z', 0, 0, tiled=True)  17.3 us
    ppermute x1, starting transfers between devices, local(): s1 = lax.ppermute(core_msg, 'core', [(0, 1), (1, 0)])  15.5 us
    all_to_all x1, blocking collectives, local(): got = lax.all_to_all(edges, 'cols', 0, 0, tiled=True)  10.1 us
    all_to_all x1, starting transfers between devices, local(): gathered = lax.all_to_all(second, ('x', 'core', 'cols'), 0, 0, tiled=True)  7.42 us
    all_to_all x1, waiting for transfers between devices, local(): gathered = lax.all_to_all(second, ('x', 'core', 'cols'), 0, 0, tiled=True)  7.17 us
    ppermute x1, waiting for transfers between devices, local(): s2 = lax.ppermute(chip_msg, ROWAX, swap)  4.53 us
    ppermute x1, starting transfers between devices, local(): s2_late = lax.ppermute(chip_late, ROWAX, swap)  4.51 us
  transfers between devices with their start and end apart: 5, of which 3 were waited for; matrix products, arithmetic and copies ran while one was open for 1% of the time, Pallas kernels for 0%

profile of v4, /device:TPU:1, one launch (start us, length us, event | category | flops | bytes accessed | tf_op | source)
XLA Modules:
  0.0 91.3 jit_solution(6550266587130610842)
XLA Ops:
  0.0 1.8 %first.1 = f32[4,72,128]{2,1,0:T(8,128)} custom-call(f32[8,2048]{1,0:T(8,128)} %b.3, f32[8,2048]{1,0:T(8,128)} %r.3, f32[8,2048]{1,0:T(8,128)} %c.3, f32[8,2048]{1,0:T(8,128)} %l.3, s32[192,128]{1,0:T(8,128)} %bitcast.2, f32[4,1024]{1,0:T(4,128)} %bitcast.4), custom_call_target="tpu_custom_call" | custom-call | tf_op jit(solution)/shard_map/first/pallas_call | solution.py:277
  1.8 0.0 copy-start
  1.8 0.0 copy-start.1
  1.9 0.0 copy-start.2
  1.9 0.0 copy-start.3
  1.9 0.0 copy-start.5
  1.9 10.1 %all_to_all.15.got = f32[4,72,128]{2,1,0:T(8,128)S(1)} all-to-all(f32[4,72,128]{2,1,0:T(8,128)} %first.1), channel_id=1, replica_groups=mesh['x'=4,'z'=32,'core'=2,'cols'=4] {'cols'}, dimensions={0} | all-to-all | bytes 294912 | tf_op jit(solution)/shard_map/all_to_all | solution.py:294
  12.0 0.0 copy-done.4
  12.0 0.0 copy-done
  12.0 0.0 copy-done.1
  12.0 0.2 rows.1
  12.2 15.5 %collective-permute-start.1 = (f32[408,128]{1,0:T(8,128)S(1)}, f32[408,128]{1,0:T(8,128)S(1)}, u32[]{:S(2)}, u32[]{:S(2)}) collective-permute-start(f32[408,128]{1,0:T(8,128)S(1)} %get-tuple-element.21), channel_id=1, source_target_pairs={{0,4},{4,0},{1,5},{5,1},{2,6},{6,2},{3,7},{7,3},{8,12},{12,8},{9,1... | collective-permute-start | bytes 626696 | tf_op jit(solution)/shard_map/ppermute | solution.py:307
  27.8 1.9 %collective-permute-start = (f32[16,2304]{1,0:T(8,128)S(1)}, f32[16,2304]{1,0:T(8,128)S(1)}, u32[]{:S(2)}, u32[]{:S(2)}) collective-permute-start(f32[16,2304]{1,0:T(8,128)S(1)} %get-tuple-element.20), channel_id=1, source_target_pairs={{4,8},{8,4},{12,16},{16,12},{20,24},{24,20},{28,32},{32,28},{36,40... | collective-permute-start | bytes 442376 | tf_op jit(solution)/shard_map/ppermute | solution.py:306
  29.7 4.5 %collective-permute-done.s2 = f32[16,2304]{1,0:T(8,128)S(1)} collective-permute-done((f32[16,2304]{1,0:T(8,128)S(1)}, f32[16,2304]{1,0:T(8,128)S(1)}, u32[]{:S(2)}, u32[]{:S(2)}) %collective-permute-start) | collective-permute-done | bytes 147488 | tf_op jit(solution)/shard_map/ppermute | solution.py:306
  34.2 0.0 collective-permute-done.1.s1
  34.2 1.3 %middle.1 = (f32[16,2304]{1,0:T(8,128)S(1)}, f32[16,2304]{1,0:T(8,128)S(1)}, f32[16,2304]{1,0:T(8,128)S(1)}, f32[16,2304]{1,0:T(8,128)S(1)}, f32[16,2304]{1,0:T(...) custom-call(f32[8,2048]{1,0:T(8,128)S(1)} %copy-done, f32[8,2048]{1,0:T(8,128)S(1)} %copy-done.1, ...), custom_call_target="tpu_custom_call" | custom-call | tf_op jit(solution)/shard_map/middle/pallas_call | solution.py:310
  35.5 17.3 %all-to-all-start.1 = ((f32[32,2,128]{2,1,0:T(2,128)}), f32[32,2,128]{2,1,0:T(2,128)S(1)}, u32[]{:S(2)}, u32[]{:S(2)}) async-start(f32[32,2,128]{2,1,0:T(2,128)} %get-tuple-element.22), calls=%async_computation.1 | async-start | bytes 65536 | tf_op jit(solution)/shard_map/all_to_all | solution.py:313
  52.8 4.5 %collective-permute-start.2 = (f32[120,128]{1,0:T(8,128)S(1)}, f32[120,128]{1,0:T(8,128)S(1)}, u32[]{:S(2)}, u32[]{:S(2)}) collective-permute-start(f32[120,128]{1,0:T(8,128)S(1)} %get-tuple-element.24), channel_id=1, source_target_pairs={{4,8},{8,4},{12,16},{16,12},{20,24},{24,20},{28,32},{32,28},{36,40... | collective-permute-start | bytes 184328 | tf_op jit(solution)/shard_map/ppermute | solution.py:314
  57.3 17.5 %all-to-all-done.1 = f32[32,2,128]{2,1,0:T(2,128)S(1)} async-done(((f32[32,2,128]{2,1,0:T(2,128)}), f32[32,2,128]{2,1,0:T(2,128)S(1)}, u32[]{:S(2)}, u32[]{:S(2)}) %all-to-all-start.1) | async-done | bytes 32800 | tf_op jit(solution)/shard_map/all_to_all | solution.py:313
  74.8 0.6 broadcast_in_dim.2
  75.5 7.4 %all-to-all-start.2 = ((f32[32,2,128]{2,1,0:T(2,128)}), f32[32,2,128]{2,1,0:T(2,128)S(1)}, u32[]{:S(2)}, u32[]{:S(2)}) async-start(f32[32,2,128]{2,1,0:T(2,128)} %broadcast_in_dim.2), calls=%async_computation.2 | async-start | bytes 65536 | tf_op jit(solution)/shard_map/all_to_all | solution.py:318
  82.9 0.0 collective-permute-done.2.s2
  82.9 7.2 %all-to-all-done.2.gathered = f32[32,2,128]{2,1,0:T(2,128)S(1)} async-done(((f32[32,2,128]{2,1,0:T(2,128)}), f32[32,2,128]{2,1,0:T(2,128)S(1)}, u32[]{:S(2)}, u32[]{:S(2)}) %all-to-all-start.2) | async-done | bytes 32800 | tf_op jit(solution)/shard_map/all_to_all | solution.py:318
  90.1 1.2 %last.1 = f32[8,2048]{1,0:T(8,128)} custom-call(f32[32,2,128]{2,1,0:T(2,128)S(1)} %all-to-all-done.2.gathered, f32[192,128]{1,0:T(8,128)S(1)} %get-tuple-element.25.mwin, f32[16,2304]{1,0:T(8,128)S(1)} %get-tuple-element.26.pre, f32[16,2304]{1,0:T(8,128)S(1)} %get-tuple-element.27.z_i, f32[16,2304]{1,0:T(8,128)S(1)} %get-tuple-element.28.wt, ...), custom_call_target="tpu_custom_call" | custom-call | tf_op jit(solution)/shard_map/last/pallas_call | solution.py:319
  (6 shorter events, 0.1 us)
Async XLA Ops:
  0.0 12.0 %copy-start.4 = (s32[1,1,192,128]{3,2,1,0:T(8,128)S(1)}, s32[1,1,192,128]{3,2,1,0:T(8,128)}, u32[]{:S(2)}) copy-start(s32[1,1,192,128]{3,2,1,0:T(8,128)} %param.10) | copy-start | bytes 294916
  1.8 10.1 %copy-start = (f32[8,2048]{1,0:T(8,128)S(1)}, f32[8,2048]{1,0:T(8,128)}, u32[]{:S(2)}) copy-start(f32[8,2048]{1,0:T(8,128)} %b.3) | copy-start | bytes 196612
  1.8 10.1 %copy-start.1 = (f32[8,2048]{1,0:T(8,128)S(1)}, f32[8,2048]{1,0:T(8,128)}, u32[]{:S(2)}) copy-start(f32[8,2048]{1,0:T(8,128)} %r.3) | copy-start | bytes 196612
  1.9 10.1 %copy-start.2 = (f32[8,2048]{1,0:T(8,128)S(1)}, f32[8,2048]{1,0:T(8,128)}, u32[]{:S(2)}) copy-start(f32[8,2048]{1,0:T(8,128)} %c.3) | copy-start | bytes 196612
  1.9 10.1 %copy-start.3 = (f32[8,2048]{1,0:T(8,128)S(1)}, f32[8,2048]{1,0:T(8,128)}, u32[]{:S(2)}) copy-start(f32[8,2048]{1,0:T(8,128)} %l.3) | copy-start | bytes 196612
  1.9 10.1 %copy-start.5 = (f32[1,4,1024]{2,1,0:T(4,128)S(1)}, f32[1,4,1024]{2,1,0:T(4,128)}, u32[]{:S(2)}) copy-start(f32[1,4,1024]{2,1,0:T(4,128)} %param.11) | copy-start | bytes 49156
  12.2 22.0 %collective-permute-start.1 = (f32[408,128]{1,0:T(8,128)S(1)}, f32[408,128]{1,0:T(8,128)S(1)}, u32[]{:S(2)}, u32[]{:S(2)}) collective-permute-start(f32[408,128]{1,0:T(8,128)S(1)} %get-tuple-element.21), channel_id=1, source_target_pairs={{0,4},{4,0},{1,5},{5,1},{2,6},{6,2},{3,7},{7,3},{8,12},{12,8},{9,1... | collective-permute-start | bytes 626696 | tf_op jit(solution)/shard_map/ppermute | solution.py:307
  27.8 6.5 %collective-permute-start = (f32[16,2304]{1,0:T(8,128)S(1)}, f32[16,2304]{1,0:T(8,128)S(1)}, u32[]{:S(2)}, u32[]{:S(2)}) collective-permute-start(f32[16,2304]{1,0:T(8,128)S(1)} %get-tuple-element.20), channel_id=1, source_target_pairs={{4,8},{8,4},{12,16},{16,12},{20,24},{24,20},{28,32},{32,28},{36,40... | collective-permute-start | bytes 442376 | tf_op jit(solution)/shard_map/ppermute | solution.py:306
  35.5 39.3 %all-to-all-start.1 = ((f32[32,2,128]{2,1,0:T(2,128)}), f32[32,2,128]{2,1,0:T(2,128)S(1)}, u32[]{:S(2)}, u32[]{:S(2)}) async-start(f32[32,2,128]{2,1,0:T(2,128)} %get-tuple-element.22), calls=%async_computation.1 | async-start | bytes 65536 | tf_op jit(solution)/shard_map/all_to_all | solution.py:313
  52.8 30.1 %collective-permute-start.2 = (f32[120,128]{1,0:T(8,128)S(1)}, f32[120,128]{1,0:T(8,128)S(1)}, u32[]{:S(2)}, u32[]{:S(2)}) collective-permute-start(f32[120,128]{1,0:T(8,128)S(1)} %get-tuple-element.24), channel_id=1, source_target_pairs={{4,8},{8,4},{12,16},{16,12},{20,24},{24,20},{28,32},{32,28},{36,40... | collective-permute-start | bytes 184328 | tf_op jit(solution)/shard_map/ppermute | solution.py:314
  75.5 14.6 %all-to-all-start.2 = ((f32[32,2,128]{2,1,0:T(2,128)}), f32[32,2,128]{2,1,0:T(2,128)S(1)}, u32[]{:S(2)}, u32[]{:S(2)}) async-start(f32[32,2,128]{2,1,0:T(2,128)} %broadcast_in_dim.2), calls=%async_computation.2 | async-start | bytes 65536 | tf_op jit(solution)/shard_map/all_to_all | solution.py:318

commit v5 on v4

--- a/solution.py
+++ b/solution.py
@@ -127,26 +127,33 @@
     return up, down
 
 
-def rows_kernel(group, b, r, c, l, agg, m, got, chip_msg, core_msg, chip_late, w, mflat):
+def rows_kernel(group, b, r, c, l, agg, m, got, chip_msg, core_msg, w, mflat):
     weights(group, agg, w)
     flatten(m, mflat)
     lower = lax.axis_index("core") == 1
     left, right = side_block(got, -1), side_block(got, 1)
     up, down = row_messages(b, r, c, l, left, right)
-    chip_msg[...] = jnp.where(lower, down, up)
-    message = jnp.where(lower, up, down)
     ww = halves(left, w, right, 4)
     half = mflat.shape[0] // 2
     mats = (left[40:], mflat[...], right[40:])
+    rows = 4 * HALO
     ncol = ww.shape[1] // LANES
-    rows = 4 * HALO
     for t in range(ncol):
-        core_msg[rows * t : rows * (t + 1), :] = message[:, t * LANES : (t + 1) * LANES]
-    late_up = [ww[0:4, t * LANES : (t + 1) * LANES] for t in range(ncol)] + [x[:half] for x in mats]
-    late_down = [ww[4:8, t * LANES : (t + 1) * LANES] for t in range(ncol)] + [x[half:] for x in mats]
-    late_up, late_down = jnp.concatenate(late_up, axis=0), jnp.concatenate(late_down, axis=0)
-    core_msg[rows * ncol :, :] = jnp.where(lower, late_up, late_down)
-    chip_late[...] = jnp.where(lower, late_down, late_up)
+        s = slice(t * LANES, (t + 1) * LANES)
+        at = slice(rows * t, rows * (t + 1))
+        core_msg[at, :] = jnp.where(lower, up[:, s], down[:, s])
+        chip_msg[at, :] = jnp.where(lower, down[:, s], up[:, s])
+    for t in range(0, ncol, 2):
+        s, e = slice(t * LANES, (t + 1) * LANES), slice((t + 1) * LANES, (t + 2) * LANES)
+        first = jnp.concatenate([ww[0:4, s], ww[0:4, e]], axis=0)
+        final = jnp.concatenate([ww[4:8, s], ww[4:8, e]], axis=0)
+        at = slice(rows * ncol + HALO * t, rows * ncol + HALO * (t + 2))
+        core_msg[at, :] = jnp.where(lower, first, final)
+        chip_msg[at, :] = jnp.where(lower, final, first)
+    for i, x in enumerate(mats):
+        at = slice((rows + HALO) * ncol + half * i, (rows + HALO) * ncol + half * (i + 1))
+        core_msg[at, :] = jnp.where(lower, x[:half], x[half:])
+        chip_msg[at, :] = jnp.where(lower, x[half:], x[:half])
 
 
 def shifted(v):
@@ -163,9 +170,9 @@
 def middle(b, r, c, l, w, got, s2, s1, pre_o, z_o, east_o, west_o, south_o, north_o, msg):
     upper = lax.axis_index("core") == 0
     left, right = side_block(got, -1), side_block(got, 1)
-    chip = s2[...]
     rows = 4 * HALO
-    pair = jnp.concatenate([s1[rows * t : rows * (t + 1), :] for t in range(chip.shape[1] // LANES)], axis=1)
+    tiles = range(b.shape[1] // LANES + 2)
+    pair, chip = [jnp.concatenate([x[rows * t : rows * (t + 1), :] for t in tiles], axis=1) for x in (s1, s2)]
     above, below = jnp.where(upper, chip, pair), jnp.where(upper, pair, chip)
     wins = []
     for i, x in enumerate((b, l, r, c)):
@@ -210,10 +217,10 @@
 def late_kernel(w, mflat, got, s1, s2, wt, mwin):
     upper = lax.axis_index("core") == 0
     left, right = side_block(got, -1), side_block(got, 1)
-    pair, chip = s1[s1.shape[0] - s2.shape[0] :, :], s2[...]
-    above, below = jnp.where(upper, chip, pair), jnp.where(upper, pair, chip)
     ww = halves(left, w, right, 4)
     ncol = ww.shape[1] // LANES
+    pair, chip = s1[4 * HALO * ncol :, :], s2[4 * HALO * ncol :, :]
+    above, below = jnp.where(upper, chip, pair), jnp.where(upper, pair, chip)
     for t in range(ncol):
         at = slice(HALO * t, HALO * (t + 1))
         s = slice(t * LANES, (t + 1) * LANES)
@@ -296,12 +303,9 @@
     swap = []
     for i in range(1, devices - 1, 2):
         swap += [(i, i + 1), (i + 1, i)]
-    late = HALO * wide // LANES + 6 * tiles
-    chip_msg, core_msg, chip_late, w, mflat = call(
-        functools.partial(rows_kernel, group),
-        [f32(4 * HALO, wide), f32(4 * HALO * wide // LANES + late, LANES), f32(late, LANES), block, f32(4 * tiles, LANES)],
-        7,
-        "rows",
+    message = f32((4 * HALO + HALO) * wide // LANES + 6 * tiles, LANES)
+    chip_msg, core_msg, w, mflat = call(
+        functools.partial(rows_kernel, group), [message, message, block, f32(4 * tiles, LANES)], 7, "rows"
     )(b, r, c, l, agg, m, got)
     s2 = lax.ppermute(chip_msg, ROWAX, swap)
     s1 = lax.ppermute(core_msg, "core", [(0, 1), (1, 0)])
@@ -311,8 +315,7 @@
         b, r, c, l, w, got, s2, s1
     )
     spread = lax.all_to_all(msg, "z", 0, 0, tiled=True)
-    s2_late = lax.ppermute(chip_late, ROWAX, swap)
-    wt, mwin = call(late_kernel, [win, f32(24 * tiles, LANES)], 5, "late")(w, mflat, got, s1, s2_late)
+    wt, mwin = call(late_kernel, [win, f32(24 * tiles, LANES)], 5, "late")(w, mflat, got, s1, s2)
     line = jnp.sum(spread, axis=0)
     second = jnp.broadcast_to(line[None], (xs * cores * cols, per_x, LANES))
     gathered = lax.all_to_all(second, ("x", "core", "cols"), 0, 0, tiled=True)

time: 91.7 us -> 89.6 us (0.977)
  blocking collectives: 10.1 us -> 51.5 us
  starting transfers between devices: 46.6 us -> 24.7 us
  waiting for transfers between devices: 29.2 us -> 8.24 us
    all_to_all x0 -> x1, blocking collectives: none -> 41.4 us  [local(): spread = lax.all_to_all(msg, 'z', 0, 0, tiled=True)]
    all_to_all x1 -> x0, waiting for transfers between devices: 17.5 us -> none  [local(): spread = lax.all_to_all(msg, 'z', 0, 0, tiled=True)]
    all_to_all x1 -> x0, starting transfers between devices: 17.3 us -> none  [local(): spread = lax.all_to_all(msg, 'z', 0, 0, tiled=True)]
    ppermute x1, starting transfers between devices: 15.5 us -> 10.6 us  [local(): s1 = lax.ppermute(core_msg, 'core', [(0, 1), (1, 0)])]
    ppermute x1, waiting for transfers between devices: 4.53 us -> 0.01 us  [local(): s2 = lax.ppermute(chip_msg, ROWAX, swap)]
    ppermute x1 -> x0, starting transfers between devices: 4.51 us -> none  [local(): s2_late = lax.ppermute(chip_late, ROWAX, swap)]
    ppermute x1, starting transfers between devices: 1.92 us -> 5.54 us  [local(): s2 = lax.ppermute(chip_msg, ROWAX, swap)]
    all_to_all x1, starting transfers between devices: 7.42 us -> 8.51 us  [local(): gathered = lax.all_to_all(second, ('x', 'core', 'cols'), 0, 0, tiled=True)]
  transfers between devices with their start and end apart: 5 -> 3, of which waited for: 3 -> 2; matrix products, arithmetic and copies ran while one was open for 1% -> 0% of each run, Pallas kernels for 0% -> 0%
where the time goes in v5:
time: 89.6 us; the launch traced here: 89.2 us
  blocking collectives  51.5 us (57%)
  starting transfers between devices  24.7 us (28%)
  waiting for transfers between devices  8.24 us (9%)
  Pallas kernels  3.95 us (4%)
    all_to_all x1, blocking collectives, local(): spread = lax.all_to_all(msg, 'z', 0, 0, tiled=True)  41.4 us
    ppermute x1, starting transfers between devices, local(): s1 = lax.ppermute(core_msg, 'core', [(0, 1), (1, 0)])  10.6 us
    all_to_all x1, blocking collectives, local(): got = lax.all_to_all(edges, 'cols', 0, 0, tiled=True)  10.1 us
    all_to_all x1, starting transfers between devices, local(): gathered = lax.all_to_all(second, ('x', 'core', 'cols'), 0, 0, tiled=True)  8.51 us
    all_to_all x1, waiting for transfers between devices, local(): gathered = lax.all_to_all(second, ('x', 'core', 'cols'), 0, 0, tiled=True)  7.18 us
    ppermute x1, starting transfers between devices, local(): s2 = lax.ppermute(chip_msg, ROWAX, swap)  5.54 us
    pallas_call x1, Pallas kernels, local(): call(functools.partial(first_kernel, group), f32(cols, 40 + 4 * tiles, LA...  1.81 us
  transfers between devices with their start and end apart: 3, of which 2 were waited for; matrix products, arithmetic and copies ran while one was open for 0% of the time, Pallas kernels for 0%

profile of v5, /device:TPU:1, one launch (start us, length us, event | category | flops | bytes accessed | tf_op | source)
XLA Modules:
  0.0 89.2 jit_solution(10750885929512552413)
XLA Ops:
  0.0 1.8 %first.1 = f32[4,72,128]{2,1,0:T(8,128)} custom-call(f32[8,2048]{1,0:T(8,128)} %b.3, f32[8,2048]{1,0:T(8,128)} %r.3, f32[8,2048]{1,0:T(8,128)} %c.3, f32[8,2048]{1,0:T(8,128)} %l.3, s32[192,128]{1,0:T(8,128)} %bitcast.2, f32[4,1024]{1,0:T(4,128)} %bitcast.4), custom_call_target="tpu_custom_call" | custom-call | tf_op jit(solution)/shard_map/first/pallas_call | solution.py:284
  1.8 0.0 copy-start
  1.8 0.0 copy-start.1
  1.8 0.0 copy-start.2
  1.9 0.0 copy-start.3
  1.9 0.0 copy-start.5
  1.9 10.1 %all_to_all.15.got = f32[4,72,128]{2,1,0:T(8,128)S(1)} all-to-all(f32[4,72,128]{2,1,0:T(8,128)} %first.1), channel_id=1, replica_groups=mesh['x'=4,'z'=32,'core'=2,'cols'=4] {'cols'}, dimensions={0} | all-to-all | bytes 294912 | tf_op jit(solution)/shard_map/all_to_all | solution.py:301
  12.0 0.0 copy-done.4
  12.0 0.0 copy-done
  12.0 0.0 copy-done.1
  12.0 0.0 copy-done.2
  12.0 0.0 copy-done.3
  12.0 0.0 copy-done.5
  12.0 0.2 rows.1
  12.2 5.5 %collective-permute-start = (f32[408,128]{1,0:T(8,128)S(1)}, f32[408,128]{1,0:T(8,128)S(1)}, u32[]{:S(2)}, u32[]{:S(2)}) collective-permute-start(f32[408,128]{1,0:T(8,128)S(1)} %get-tuple-element.19), channel_id=1, source_target_pairs={{4,8},{8,4},{12,16},{16,12},{20,24},{24,20},{28,32},{32,28},{36,40... | collective-permute-start | bytes 626696 | tf_op jit(solution)/shard_map/ppermute | solution.py:310
  17.8 10.6 %collective-permute-start.1 = (f32[408,128]{1,0:T(8,128)S(1)}, f32[408,128]{1,0:T(8,128)S(1)}, u32[]{:S(2)}, u32[]{:S(2)}) collective-permute-start(f32[408,128]{1,0:T(8,128)S(1)} %get-tuple-element.20), channel_id=1, source_target_pairs={{0,4},{4,0},{1,5},{5,1},{2,6},{6,2},{3,7},{7,3},{8,12},{12,8},{9,1... | collective-permute-start | bytes 626696 | tf_op jit(solution)/shard_map/ppermute | solution.py:311
  28.4 0.0 collective-permute-done.s2
  28.4 1.1 %collective-permute-done.1.s1 = f32[408,128]{1,0:T(8,128)S(1)} collective-permute-done((f32[408,128]{1,0:T(8,128)S(1)}, f32[408,128]{1,0:T(8,128)S(1)}, u32[]{:S(2)}, u32[]{:S(2)}) %collective-permute-start.1) | collective-permute-done | bytes 208928 | tf_op jit(solution)/shard_map/ppermute | solution.py:311
  29.5 0.7 middle.1
  30.2 41.4 %all_to_all.16 = f32[32,2,128]{2,1,0:T(2,128)S(1)} all-to-all(f32[32,2,128]{2,1,0:T(2,128)S(1)} %get-tuple-element.21), channel_id=1, replica_groups=mesh['x'=4,'z'=32,'core'=2,'cols'=4] {'z'}, dimensions={0} | all-to-all | bytes 65536 | tf_op jit(solution)/shard_map/all_to_all | solution.py:317
  71.6 0.6 broadcast_in_dim.2
  72.2 8.5 %all-to-all-start.2 = ((f32[32,2,128]{2,1,0:T(2,128)}), f32[32,2,128]{2,1,0:T(2,128)S(1)}, u32[]{:S(2)}, u32[]{:S(2)}) async-start(f32[32,2,128]{2,1,0:T(2,128)} %broadcast_in_dim.2), calls=%async_computation.2 | async-start | bytes 65536 | tf_op jit(solution)/shard_map/all_to_all | solution.py:321
  80.8 7.2 %all-to-all-done.2.gathered = f32[32,2,128]{2,1,0:T(2,128)S(1)} async-done(((f32[32,2,128]{2,1,0:T(2,128)}), f32[32,2,128]{2,1,0:T(2,128)S(1)}, u32[]{:S(2)}, u32[]{:S(2)}) %all-to-all-start.2) | async-done | bytes 32800 | tf_op jit(solution)/shard_map/all_to_all | solution.py:321
  88.0 1.2 %last.1 = f32[8,2048]{1,0:T(8,128)} custom-call(f32[32,2,128]{2,1,0:T(2,128)S(1)} %all-to-all-done.2.gathered, f32[192,128]{1,0:T(8,128)S(1)} %get-tuple-element.23.mwin, f32[16,2304]{1,0:T(8,128)S(1)} %get-tuple-element.24.pre, f32[16,2304]{1,0:T(8,128)S(1)} %get-tuple-element.25.z_i, f32[16,2304]{1,0:T(8,128)S(1)} %get-tuple-element.26.wt, ...), custom_call_target="tpu_custom_call" | custom-call | tf_op jit(solution)/shard_map/last/pallas_call | solution.py:322
  (3 shorter events, 0.1 us)
Async XLA Ops:
  0.0 12.0 %copy-start.4 = (s32[1,1,192,128]{3,2,1,0:T(8,128)S(1)}, s32[1,1,192,128]{3,2,1,0:T(8,128)}, u32[]{:S(2)}) copy-start(s32[1,1,192,128]{3,2,1,0:T(8,128)} %param.10) | copy-start | bytes 294916
  1.8 10.1 %copy-start = (f32[8,2048]{1,0:T(8,128)S(1)}, f32[8,2048]{1,0:T(8,128)}, u32[]{:S(2)}) copy-start(f32[8,2048]{1,0:T(8,128)} %b.3) | copy-start | bytes 196612
  1.8 10.1 %copy-start.1 = (f32[8,2048]{1,0:T(8,128)S(1)}, f32[8,2048]{1,0:T(8,128)}, u32[]{:S(2)}) copy-start(f32[8,2048]{1,0:T(8,128)} %r.3) | copy-start | bytes 196612
  1.8 10.1 %copy-start.2 = (f32[8,2048]{1,0:T(8,128)S(1)}, f32[8,2048]{1,0:T(8,128)}, u32[]{:S(2)}) copy-start(f32[8,2048]{1,0:T(8,128)} %c.3) | copy-start | bytes 196612
  1.9 10.1 %copy-start.3 = (f32[8,2048]{1,0:T(8,128)S(1)}, f32[8,2048]{1,0:T(8,128)}, u32[]{:S(2)}) copy-start(f32[8,2048]{1,0:T(8,128)} %l.3) | copy-start | bytes 196612
  1.9 10.1 %copy-start.5 = (f32[1,4,1024]{2,1,0:T(4,128)S(1)}, f32[1,4,1024]{2,1,0:T(4,128)}, u32[]{:S(2)}) copy-start(f32[1,4,1024]{2,1,0:T(4,128)} %param.11) | copy-start | bytes 49156
  12.2 16.2 %collective-permute-start = (f32[408,128]{1,0:T(8,128)S(1)}, f32[408,128]{1,0:T(8,128)S(1)}, u32[]{:S(2)}, u32[]{:S(2)}) collective-permute-start(f32[408,128]{1,0:T(8,128)S(1)} %get-tuple-element.19), channel_id=1, source_target_pairs={{4,8},{8,4},{12,16},{16,12},{20,24},{24,20},{28,32},{32,28},{36,40... | collective-permute-start | bytes 626696 | tf_op jit(solution)/shard_map/ppermute | solution.py:310
  17.8 11.7 %collective-permute-start.1 = (f32[408,128]{1,0:T(8,128)S(1)}, f32[408,128]{1,0:T(8,128)S(1)}, u32[]{:S(2)}, u32[]{:S(2)}) collective-permute-start(f32[408,128]{1,0:T(8,128)S(1)} %get-tuple-element.20), channel_id=1, source_target_pairs={{0,4},{4,0},{1,5},{5,1},{2,6},{6,2},{3,7},{7,3},{8,12},{12,8},{9,1... | collective-permute-start | bytes 626696 | tf_op jit(solution)/shard_map/ppermute | solution.py:311
  72.2 15.7 %all-to-all-start.2 = ((f32[32,2,128]{2,1,0:T(2,128)}), f32[32,2,128]{2,1,0:T(2,128)S(1)}, u32[]{:S(2)}, u32[]{:S(2)}) async-start(f32[32,2,128]{2,1,0:T(2,128)} %broadcast_in_dim.2), calls=%async_computation.2 | async-start | bytes 65536 | tf_op jit(solution)/shard_map/all_to_all | solution.py:321

commit v6 on v5

--- a/solution.py
+++ b/solution.py
@@ -205,13 +205,29 @@
     for ref, value in zip((east_o, west_o, south_o, north_o), coef):
         ref[...] = value
     total = jnp.sum(part, axis=1, keepdims=True)
-    place = (lax.axis_index("z") * 2 + lax.axis_index("core")) * 4
+    place = lax.axis_index("z") * 4
     lane = lax.broadcasted_iota(jnp.int32, (8, LANES), 1)
     row = lax.broadcasted_iota(jnp.int32, (8, LANES), 0)
-    spread = jnp.where(lane == lax.rem(place, LANES) + row // 2, total, 0.0)
-    line = jnp.sum(spread, axis=0, keepdims=True)
-    rows = lax.broadcasted_iota(jnp.int32, (msg.shape[1], LANES), 0)
-    msg[...] = jnp.broadcast_to(jnp.where(rows == place // LANES, line, 0.0)[None], msg.shape)
+    spread = jnp.where(lane == place + row // 2, total, 0.0)
+    msg[...] = jnp.broadcast_to(jnp.sum(spread, axis=0, keepdims=True)[None], msg.shape)
+
+
+def reordered(m):
+    n = m.shape[0]
+    i = lax.broadcasted_iota(jnp.int32, (LANES, LANES), 0)
+    o = lax.broadcasted_iota(jnp.int32, (LANES, LANES), 1)
+    source = (o % 64) // 4 * 8 + o % 4
+
+    def pick(rows, core, high):
+        chosen = jnp.logical_and(o // 64 == high, i == source + 4 * core)
+        return jnp.dot(
+            rows, chosen.astype(jnp.float32), precision=lax.Precision.HIGHEST, preferred_element_type=jnp.float32
+        )
+
+    even = pick(m, 0, 0) + pick(pltpu.roll(m, n - 1, 0), 0, 1)
+    odd = pick(pltpu.roll(m, 1, 0), 1, 0) + pick(m, 1, 1)
+    row = lax.broadcasted_iota(jnp.int32, m.shape, 0)
+    return jnp.where(row % 2 == 0, even, odd)
 
 
 def late_kernel(w, mflat, got, s1, s2, wt, mwin):
@@ -226,11 +242,11 @@
         s = slice(t * LANES, (t + 1) * LANES)
         wt[:, s] = jnp.concatenate([ww[:, s], below[at], above[at]], axis=0)
     half = mflat.shape[0] // 2
+    parts = []
     for i, mine in enumerate((left[40:], mflat[...], right[40:])):
         at = slice(HALO * ncol + half * i, HALO * ncol + half * (i + 1))
-        mwin[4 * half * i : 4 * half * i + half, :] = above[at]
-        mwin[4 * half * i + half : 4 * half * i + 3 * half, :] = mine
-        mwin[4 * half * i + 3 * half : 4 * half * (i + 1), :] = below[at]
+        parts += [above[at], mine, below[at]]
+    mwin[...] = reordered(jnp.concatenate(parts, axis=0))
 
 
 def last(xs, gathered, mwin, pre, z_i, wt, east, west, south, north, out):
@@ -240,10 +256,7 @@
     me = lax.axis_index("cols")
 
     def corrections(group, mats):
-        v = []
-        for x in range(xs):
-            v.append(gathered[(2 * x) * ncols + group] + gathered[(2 * x + 1) * ncols + group])
-        v = jnp.concatenate(v, axis=0)
+        v = jnp.concatenate([gathered[at * ncols + group] for at in range(2 * xs)], axis=0)
         lines = []
         for m in mats[2:] + mats[:2]:
             p = jnp.sum(m * v, axis=0, keepdims=True)
@@ -309,15 +322,14 @@
     )(b, r, c, l, agg, m, got)
     s2 = lax.ppermute(chip_msg, ROWAX, swap)
     s1 = lax.ppermute(core_msg, "core", [(0, 1), (1, 0)])
-    per_x = max(1, zs * cores * 4 // LANES)
     win = f32(WROWS, wide)
-    pre, z, east, west, south, north, msg = call(middle, [win] * 6 + [f32(zs, per_x, LANES)], 8, "middle")(
+    pre, z, east, west, south, north, msg = call(middle, [win] * 6 + [f32(zs, 1, LANES)], 8, "middle")(
         b, r, c, l, w, got, s2, s1
     )
     spread = lax.all_to_all(msg, "z", 0, 0, tiled=True)
     wt, mwin = call(late_kernel, [win, f32(24 * tiles, LANES)], 5, "late")(w, mflat, got, s1, s2)
     line = jnp.sum(spread, axis=0)
-    second = jnp.broadcast_to(line[None], (xs * cores * cols, per_x, LANES))
+    second = jnp.broadcast_to(line[None], (xs * cores * cols, 1, LANES))
     gathered = lax.all_to_all(second, ("x", "core", "cols"), 0, 0, tiled=True)
     return call(functools.partial(last, xs), block, 9, "last")(
         gathered, mwin, pre, z, wt, east, west, south, north

time: 89.6 us -> 88.5 us (0.988)
  transfers between devices with their start and end apart: 3 -> 3, of which waited for: 2 -> 2; matrix products, arithmetic and copies ran while one was open for 0% -> 0% of each run, Pallas kernels for 0% -> 1%
where the time goes in v6:
time: 88.5 us; the launch traced here: 88.1 us
  blocking collectives  50.7 us (57%)
  starting transfers between devices  24.7 us (28%)
  waiting for transfers between devices  7.4 us (8%)
  Pallas kernels  4.41 us (5%)
    all_to_all x1, blocking collectives, local(): spread = lax.all_to_all(msg, 'z', 0, 0, tiled=True)  40.6 us
    ppermute x1, starting transfers between devices, local(): s1 = lax.ppermute(core_msg, 'core', [(0, 1), (1, 0)])  10.6 us
    all_to_all x1, blocking collectives, local(): got = lax.all_to_all(edges, 'cols', 0, 0, tiled=True)  10.1 us
    all_to_all x1, starting transfers between devices, local(): gathered = lax.all_to_all(second, ('x', 'core', 'cols'), 0, 0, tiled=True)  8.56 us
    all_to_all x1, waiting for transfers between devices, local(): gathered = lax.all_to_all(second, ('x', 'core', 'cols'), 0, 0, tiled=True)  6.35 us
    ppermute x1, starting transfers between devices, local(): s2 = lax.ppermute(chip_msg, ROWAX, swap)  5.54 us
    pallas_call x1, Pallas kernels, local(): call(functools.partial(first_kernel, group), f32(cols, 40 + 4 * tiles, LA...  1.81 us
  transfers between devices with their start and end apart: 3, of which 2 were waited for; matrix products, arithmetic and copies ran while one was open for 0% of the time, Pallas kernels for 1%

profile of v6, /device:TPU:1, one launch (start us, length us, event | category | flops | bytes accessed | tf_op | source)
XLA Modules:
  0.0 88.1 jit_solution(17386743311814604920)
XLA Ops:
  0.0 1.8 %first.1 = f32[4,72,128]{2,1,0:T(8,128)} custom-call(f32[8,2048]{1,0:T(8,128)} %b.3, f32[8,2048]{1,0:T(8,128)} %r.3, f32[8,2048]{1,0:T(8,128)} %c.3, f32[8,2048]{1,0:T(8,128)} %l.3, s32[192,128]{1,0:T(8,128)} %bitcast.2, f32[4,1024]{1,0:T(4,128)} %bitcast.4), custom_call_target="tpu_custom_call" | custom-call | tf_op jit(solution)/shard_map/first/pallas_call | solution.py:297
  1.8 0.0 copy-start
  1.8 0.0 copy-start.1
  1.8 0.0 copy-start.2
  1.9 0.0 copy-start.3
  1.9 0.0 copy-start.5
  1.9 10.1 %all_to_all.15.got = f32[4,72,128]{2,1,0:T(8,128)S(1)} all-to-all(f32[4,72,128]{2,1,0:T(8,128)} %first.1), channel_id=1, replica_groups=mesh['x'=4,'z'=32,'core'=2,'cols'=4] {'cols'}, dimensions={0} | all-to-all | bytes 294912 | tf_op jit(solution)/shard_map/all_to_all | solution.py:314
  12.0 0.0 copy-done.4
  12.0 0.0 copy-done
  12.0 0.0 copy-done.1
  12.0 0.0 copy-done.2
  12.0 0.2 rows.1
  12.2 5.5 %collective-permute-start = (f32[408,128]{1,0:T(8,128)S(1)}, f32[408,128]{1,0:T(8,128)S(1)}, u32[]{:S(2)}, u32[]{:S(2)}) collective-permute-start(f32[408,128]{1,0:T(8,128)S(1)} %get-tuple-element.19), channel_id=1, source_target_pairs={{4,8},{8,4},{12,16},{16,12},{20,24},{24,20},{28,32},{32,28},{36,40... | collective-permute-start | bytes 626696 | tf_op jit(solution)/shard_map/ppermute | solution.py:323
  17.8 10.6 %collective-permute-start.1 = (f32[408,128]{1,0:T(8,128)S(1)}, f32[408,128]{1,0:T(8,128)S(1)}, u32[]{:S(2)}, u32[]{:S(2)}) collective-permute-start(f32[408,128]{1,0:T(8,128)S(1)} %get-tuple-element.20), channel_id=1, source_target_pairs={{0,4},{4,0},{1,5},{5,1},{2,6},{6,2},{3,7},{7,3},{8,12},{12,8},{9,1... | collective-permute-start | bytes 626696 | tf_op jit(solution)/shard_map/ppermute | solution.py:324
  28.4 0.0 collective-permute-done.s2
  28.4 1.1 %collective-permute-done.1.s1 = f32[408,128]{1,0:T(8,128)S(1)} collective-permute-done((f32[408,128]{1,0:T(8,128)S(1)}, f32[408,128]{1,0:T(8,128)S(1)}, u32[]{:S(2)}, u32[]{:S(2)}) %collective-permute-start.1) | collective-permute-done | bytes 208928 | tf_op jit(solution)/shard_map/ppermute | solution.py:324
  29.5 0.7 middle.1
  30.2 40.6 %all_to_all.16 = f32[32,1,128]{2,1,0:T(1,128)S(1)} all-to-all(f32[32,1,128]{2,1,0:T(1,128)S(1)} %get-tuple-element.21), channel_id=1, replica_groups=mesh['x'=4,'z'=32,'core'=2,'cols'=4] {'z'}, dimensions={0} | all-to-all | bytes 32768 | tf_op jit(solution)/shard_map/all_to_all | solution.py:329
  70.8 0.1 reduce_sum.9
  70.9 0.6 broadcast_in_dim.2
  71.5 8.6 %all-to-all-start.2 = ((f32[32,1,128]{2,1,0:T(1,128)}), f32[32,1,128]{2,1,0:T(1,128)S(1)}, u32[]{:S(2)}, u32[]{:S(2)}) async-start(f32[32,1,128]{2,1,0:T(1,128)} %broadcast_in_dim.2), calls=%async_computation.2 | async-start | bytes 32768 | tf_op jit(solution)/shard_map/all_to_all | solution.py:333
  80.0 0.5 late.1
  80.5 6.3 %all-to-all-done.2.gathered = f32[32,1,128]{2,1,0:T(1,128)S(1)} async-done(((f32[32,1,128]{2,1,0:T(1,128)}), f32[32,1,128]{2,1,0:T(1,128)S(1)}, u32[]{:S(2)}, u32[]{:S(2)}) %all-to-all-start.2) | async-done | bytes 16416 | tf_op jit(solution)/shard_map/all_to_all | solution.py:333
  86.9 1.2 %last.1 = f32[8,2048]{1,0:T(8,128)} custom-call(f32[32,1,128]{2,1,0:T(1,128)S(1)} %all-to-all-done.2.gathered, f32[192,128]{1,0:T(8,128)S(1)} %get-tuple-element.23.mwin, f32[16,2304]{1,0:T(8,128)S(1)} %get-tuple-element.24.pre, f32[16,2304]{1,0:T(8,128)S(1)} %get-tuple-element.25.z_i, f32[16,2304]{1,0:T(8,128)S(1)} %get-tuple-element.26.wt, ...), custom_call_target="tpu_custom_call" | custom-call | tf_op jit(solution)/shard_map/last/pallas_call | solution.py:334
  (3 shorter events, 0.0 us)
Async XLA Ops:
  0.0 12.0 %copy-start.4 = (s32[1,1,192,128]{3,2,1,0:T(8,128)S(1)}, s32[1,1,192,128]{3,2,1,0:T(8,128)}, u32[]{:S(2)}) copy-start(s32[1,1,192,128]{3,2,1,0:T(8,128)} %param.10) | copy-start | bytes 294916
  1.8 10.1 %copy-start = (f32[8,2048]{1,0:T(8,128)S(1)}, f32[8,2048]{1,0:T(8,128)}, u32[]{:S(2)}) copy-start(f32[8,2048]{1,0:T(8,128)} %b.3) | copy-start | bytes 196612
  1.8 10.1 %copy-start.1 = (f32[8,2048]{1,0:T(8,128)S(1)}, f32[8,2048]{1,0:T(8,128)}, u32[]{:S(2)}) copy-start(f32[8,2048]{1,0:T(8,128)} %r.3) | copy-start | bytes 196612
  1.8 10.1 %copy-start.2 = (f32[8,2048]{1,0:T(8,128)S(1)}, f32[8,2048]{1,0:T(8,128)}, u32[]{:S(2)}) copy-start(f32[8,2048]{1,0:T(8,128)} %c.3) | copy-start | bytes 196612
  1.9 10.1 %copy-start.3 = (f32[8,2048]{1,0:T(8,128)S(1)}, f32[8,2048]{1,0:T(8,128)}, u32[]{:S(2)}) copy-start(f32[8,2048]{1,0:T(8,128)} %l.3) | copy-start | bytes 196612
  1.9 10.1 %copy-start.5 = (f32[1,4,1024]{2,1,0:T(4,128)S(1)}, f32[1,4,1024]{2,1,0:T(4,128)}, u32[]{:S(2)}) copy-start(f32[1,4,1024]{2,1,0:T(4,128)} %param.11) | copy-start | bytes 49156
  12.2 16.2 %collective-permute-start = (f32[408,128]{1,0:T(8,128)S(1)}, f32[408,128]{1,0:T(8,128)S(1)}, u32[]{:S(2)}, u32[]{:S(2)}) collective-permute-start(f32[408,128]{1,0:T(8,128)S(1)} %get-tuple-element.19), channel_id=1, source_target_pairs={{4,8},{8,4},{12,16},{16,12},{20,24},{24,20},{28,32},{32,28},{36,40... | collective-permute-start | bytes 626696 | tf_op jit(solution)/shard_map/ppermute | solution.py:323
  17.8 11.7 %collective-permute-start.1 = (f32[408,128]{1,0:T(8,128)S(1)}, f32[408,128]{1,0:T(8,128)S(1)}, u32[]{:S(2)}, u32[]{:S(2)}) collective-permute-start(f32[408,128]{1,0:T(8,128)S(1)} %get-tuple-element.20), channel_id=1, source_target_pairs={{0,4},{4,0},{1,5},{5,1},{2,6},{6,2},{3,7},{7,3},{8,12},{12,8},{9,1... | collective-permute-start | bytes 626696 | tf_op jit(solution)/shard_map/ppermute | solution.py:324
  71.5 15.4 %all-to-all-start.2 = ((f32[32,1,128]{2,1,0:T(1,128)}), f32[32,1,128]{2,1,0:T(1,128)S(1)}, u32[]{:S(2)}, u32[]{:S(2)}) async-start(f32[32,1,128]{2,1,0:T(1,128)} %broadcast_in_dim.2), calls=%async_computation.2 | async-start | bytes 32768 | tf_op jit(solution)/shard_map/all_to_all | solution.py:333

commit v7 on v6

--- a/solution.py
+++ b/solution.py
@@ -16,6 +16,7 @@
 RHO2 = 1.0 / (2.0 * THETA / DELTA - RHO1)
 LANES = 128
 HALO = 4
+EDGE = 8
 WROWS = 16
 ROWAX = ("x", "z", "core")
 VMEM_LIMIT = 48 * 1024 * 1024
@@ -84,9 +85,16 @@
     weights(group, agg_v, w_v)
     flatten(m_v, mflat)
     refs = (b_v, l_v, r_v, c_v, w_v)
-    mine = mflat[...]
-    left = jnp.concatenate([x[:, 0:LANES] for x in refs] + [mine], axis=0)
-    right = jnp.concatenate([x[:, n - LANES : n] for x in refs] + [mine], axis=0)
+    lane = lax.broadcasted_iota(jnp.int32, (8, LANES), 1)
+
+    def packed(at, shift):
+        out = jnp.zeros((8, LANES), jnp.float32)
+        for i, x in enumerate(refs):
+            moved = pltpu.roll(x[:, at : at + LANES], (shift + EDGE * i) % LANES, 1)
+            out = jnp.where(lane // EDGE == i, moved, out)
+        return jnp.concatenate([out, mflat[...]], axis=0)
+
+    left, right = packed(0, 0), packed(n - LANES, EDGE)
     me = lax.axis_index("cols")
     for c in range(edges.shape[0]):
         edges[c] = jnp.where(me > c, left, right)
@@ -96,7 +104,14 @@
     cols = lax.axis_size("cols")
     c = lax.axis_index("cols") + step
     ok = jnp.logical_and(c >= 0, c < cols)
-    return jnp.where(ok, got[jnp.clip(c, 0, cols - 1)], 0.0)
+    block = jnp.where(ok, got[jnp.clip(c, 0, cols - 1)], 0.0)
+    lane = lax.broadcasted_iota(jnp.int32, (8, LANES), 1)
+    start = LANES - EDGE if step < 0 else 0
+    near = jnp.logical_and(lane >= start, lane < start + EDGE)
+    out = []
+    for i in range(5):
+        out.append(jnp.where(near, pltpu.roll(block[0:8], (start - EDGE * i) % LANES, 1), 0.0))
+    return jnp.concatenate(out + [block[8:]], axis=0)
 
 
 def widened(left, own, right):
@@ -296,7 +311,7 @@
     block = f32(8, width)
     edges = call(
         functools.partial(first_kernel, group),
-        f32(cols, 40 + 4 * tiles, LANES),
+        f32(cols, 8 + 4 * tiles, LANES),
         6,
         "first",
         space=pltpu.HBM,

time: 88.5 us -> 88.3 us (level)
  no operation moved by 1% of the time
where the time goes in v7:
time: 88.3 us; the launch traced here: 87.9 us
  blocking collectives  50.4 us (57%)
  starting transfers between devices  24.7 us (28%)
  waiting for transfers between devices  7.4 us (8%)
  Pallas kernels  4.6 us (5%)
    all_to_all x1, blocking collectives, local(): spread = lax.all_to_all(msg, 'z', 0, 0, tiled=True)  40.7 us
    ppermute x1, starting transfers between devices, local(): s1 = lax.ppermute(core_msg, 'core', [(0, 1), (1, 0)])  10.6 us
    all_to_all x1, blocking collectives, local(): got = lax.all_to_all(edges, 'cols', 0, 0, tiled=True)  9.72 us
    all_to_all x1, starting transfers between devices, local(): gathered = lax.all_to_all(second, ('x', 'core', 'cols'), 0, 0, tiled=True)  8.56 us
    all_to_all x1, waiting for transfers between devices, local(): gathered = lax.all_to_all(second, ('x', 'core', 'cols'), 0, 0, tiled=True)  6.34 us
    ppermute x1, starting transfers between devices, local(): s2 = lax.ppermute(chip_msg, ROWAX, swap)  5.54 us
    pallas_call x1, Pallas kernels, local(): call(functools.partial(first_kernel, group), f32(cols, 8 + 4 * tiles, LAN...  1.86 us
  transfers between devices with their start and end apart: 3, of which 2 were waited for; matrix products, arithmetic and copies ran while one was open for 0% of the time, Pallas kernels for 1%

profile of v7, /device:TPU:1, one launch (start us, length us, event | category | flops | bytes accessed | tf_op | source)
XLA Modules:
  0.0 87.9 jit_solution(17786593121969425320)
XLA Ops:
  0.0 1.9 %first.1 = f32[4,40,128]{2,1,0:T(8,128)} custom-call(f32[8,2048]{1,0:T(8,128)} %b.3, f32[8,2048]{1,0:T(8,128)} %r.3, f32[8,2048]{1,0:T(8,128)} %c.3, f32[8,2048]{1,0:T(8,128)} %l.3, s32[192,128]{1,0:T(8,128)} %bitcast.2, f32[4,1024]{1,0:T(4,128)} %bitcast.4), custom_call_target="tpu_custom_call" | custom-call | tf_op jit(solution)/shard_map/first/pallas_call | solution.py:312
  1.9 0.0 copy-start
  1.9 0.0 copy-start.1
  1.9 0.0 copy-start.5
  1.9 9.7 %all_to_all.15.got = f32[4,40,128]{2,1,0:T(8,128)S(1)} all-to-all(f32[4,40,128]{2,1,0:T(8,128)} %first.1), channel_id=1, replica_groups=mesh['x'=4,'z'=32,'core'=2,'cols'=4] {'cols'}, dimensions={0} | all-to-all | bytes 163840 | tf_op jit(solution)/shard_map/all_to_all | solution.py:329
  11.6 0.0 copy-done.2
  11.6 0.0 copy-done.3
  11.6 0.0 copy-done.4
  11.6 0.0 copy-done
  11.7 0.0 copy-done.1
  11.7 0.0 copy-done.5
  11.7 0.3 rows.1
  12.0 5.5 %collective-permute-start = (f32[408,128]{1,0:T(8,128)S(1)}, f32[408,128]{1,0:T(8,128)S(1)}, u32[]{:S(2)}, u32[]{:S(2)}) collective-permute-start(f32[408,128]{1,0:T(8,128)S(1)} %get-tuple-element.19), channel_id=1, source_target_pairs={{4,8},{8,4},{12,16},{16,12},{20,24},{24,20},{28,32},{32,28},{36,40... | collective-permute-start | bytes 626696 | tf_op jit(solution)/shard_map/ppermute | solution.py:338
  17.5 10.6 %collective-permute-start.1 = (f32[408,128]{1,0:T(8,128)S(1)}, f32[408,128]{1,0:T(8,128)S(1)}, u32[]{:S(2)}, u32[]{:S(2)}) collective-permute-start(f32[408,128]{1,0:T(8,128)S(1)} %get-tuple-element.20), channel_id=1, source_target_pairs={{0,4},{4,0},{1,5},{5,1},{2,6},{6,2},{3,7},{7,3},{8,12},{12,8},{9,1... | collective-permute-start | bytes 626696 | tf_op jit(solution)/shard_map/ppermute | solution.py:339
  28.1 0.0 collective-permute-done.s2
  28.1 1.1 %collective-permute-done.1.s1 = f32[408,128]{1,0:T(8,128)S(1)} collective-permute-done((f32[408,128]{1,0:T(8,128)S(1)}, f32[408,128]{1,0:T(8,128)S(1)}, u32[]{:S(2)}, u32[]{:S(2)}) %collective-permute-start.1) | collective-permute-done | bytes 208928 | tf_op jit(solution)/shard_map/ppermute | solution.py:339
  29.2 0.8 middle.1
  29.9 40.7 %all_to_all.16 = f32[32,1,128]{2,1,0:T(1,128)S(1)} all-to-all(f32[32,1,128]{2,1,0:T(1,128)S(1)} %get-tuple-element.21), channel_id=1, replica_groups=mesh['x'=4,'z'=32,'core'=2,'cols'=4] {'z'}, dimensions={0} | all-to-all | bytes 32768 | tf_op jit(solution)/shard_map/all_to_all | solution.py:344
  70.6 0.1 reduce_sum.9
  70.7 0.6 broadcast_in_dim.2
  71.3 8.6 %all-to-all-start.2 = ((f32[32,1,128]{2,1,0:T(1,128)}), f32[32,1,128]{2,1,0:T(1,128)S(1)}, u32[]{:S(2)}, u32[]{:S(2)}) async-start(f32[32,1,128]{2,1,0:T(1,128)} %broadcast_in_dim.2), calls=%async_computation.2 | async-start | bytes 32768 | tf_op jit(solution)/shard_map/all_to_all | solution.py:348
  79.9 0.5 late.1
  80.4 6.3 %all-to-all-done.2.gathered = f32[32,1,128]{2,1,0:T(1,128)S(1)} async-done(((f32[32,1,128]{2,1,0:T(1,128)}), f32[32,1,128]{2,1,0:T(1,128)S(1)}, u32[]{:S(2)}, u32[]{:S(2)}) %all-to-all-start.2) | async-done | bytes 16416 | tf_op jit(solution)/shard_map/all_to_all | solution.py:348
  86.7 1.2 %last.1 = f32[8,2048]{1,0:T(8,128)} custom-call(f32[32,1,128]{2,1,0:T(1,128)S(1)} %all-to-all-done.2.gathered, f32[192,128]{1,0:T(8,128)S(1)} %get-tuple-element.23.mwin, f32[16,2304]{1,0:T(8,128)S(1)} %get-tuple-element.24.pre, f32[16,2304]{1,0:T(8,128)S(1)} %get-tuple-element.25.z_i, f32[16,2304]{1,0:T(8,128)S(1)} %get-tuple-element.26.wt, ...), custom_call_target="tpu_custom_call" | custom-call | tf_op jit(solution)/shard_map/last/pallas_call | solution.py:349
  (3 shorter events, 0.0 us)
Async XLA Ops:
  0.0 11.6 %copy-start.2 = (f32[8,2048]{1,0:T(8,128)S(1)}, f32[8,2048]{1,0:T(8,128)}, u32[]{:S(2)}) copy-start(f32[8,2048]{1,0:T(8,128)} %c.3) | copy-start | bytes 196612
  0.0 11.6 %copy-start.3 = (f32[8,2048]{1,0:T(8,128)S(1)}, f32[8,2048]{1,0:T(8,128)}, u32[]{:S(2)}) copy-start(f32[8,2048]{1,0:T(8,128)} %l.3) | copy-start | bytes 196612
  0.0 11.6 %copy-start.4 = (s32[1,1,192,128]{3,2,1,0:T(8,128)S(1)}, s32[1,1,192,128]{3,2,1,0:T(8,128)}, u32[]{:S(2)}) copy-start(s32[1,1,192,128]{3,2,1,0:T(8,128)} %param.10) | copy-start | bytes 294916
  1.9 9.8 %copy-start = (f32[8,2048]{1,0:T(8,128)S(1)}, f32[8,2048]{1,0:T(8,128)}, u32[]{:S(2)}) copy-start(f32[8,2048]{1,0:T(8,128)} %b.3) | copy-start | bytes 196612
  1.9 9.8 %copy-start.1 = (f32[8,2048]{1,0:T(8,128)S(1)}, f32[8,2048]{1,0:T(8,128)}, u32[]{:S(2)}) copy-start(f32[8,2048]{1,0:T(8,128)} %r.3) | copy-start | bytes 196612
  1.9 9.8 %copy-start.5 = (f32[1,4,1024]{2,1,0:T(4,128)S(1)}, f32[1,4,1024]{2,1,0:T(4,128)}, u32[]{:S(2)}) copy-start(f32[1,4,1024]{2,1,0:T(4,128)} %param.11) | copy-start | bytes 49156
  12.0 16.2 %collective-permute-start = (f32[408,128]{1,0:T(8,128)S(1)}, f32[408,128]{1,0:T(8,128)S(1)}, u32[]{:S(2)}, u32[]{:S(2)}) collective-permute-start(f32[408,128]{1,0:T(8,128)S(1)} %get-tuple-element.19), channel_id=1, source_target_pairs={{4,8},{8,4},{12,16},{16,12},{20,24},{24,20},{28,32},{32,28},{36,40... | collective-permute-start | bytes 626696 | tf_op jit(solution)/shard_map/ppermute | solution.py:338
  17.5 11.7 %collective-permute-start.1 = (f32[408,128]{1,0:T(8,128)S(1)}, f32[408,128]{1,0:T(8,128)S(1)}, u32[]{:S(2)}, u32[]{:S(2)}) collective-permute-start(f32[408,128]{1,0:T(8,128)S(1)} %get-tuple-element.20), channel_id=1, source_target_pairs={{0,4},{4,0},{1,5},{5,1},{2,6},{6,2},{3,7},{7,3},{8,12},{12,8},{9,1... | collective-permute-start | bytes 626696 | tf_op jit(solution)/shard_map/ppermute | solution.py:339
  71.3 15.4 %all-to-all-start.2 = ((f32[32,1,128]{2,1,0:T(1,128)}), f32[32,1,128]{2,1,0:T(1,128)S(1)}, u32[]{:S(2)}, u32[]{:S(2)}) async-start(f32[32,1,128]{2,1,0:T(1,128)} %broadcast_in_dim.2), calls=%async_computation.2 | async-start | bytes 32768 | tf_op jit(solution)/shard_map/all_to_all | solution.py:348

commit v8 on v7

--- a/solution.py
+++ b/solution.py
@@ -64,6 +64,7 @@
     for k in range(4):
         for t in range(tiles):
             mflat[k * tiles + t : k * tiles + t + 1, :] = m[k : k + 1, t * LANES : (t + 1) * LANES]
+    mflat[...] = reordered(mflat[...])
 
 
 def first_kernel(group, rhs, cr, cc, lk, agg, m, edges, b_v, r_v, c_v, l_v, agg_v, m_v, w_v, mflat, sems):
@@ -182,7 +183,8 @@
     return v - east * e - west * w - south * s - north * n
 
 
-def middle(b, r, c, l, w, got, s2, s1, pre_o, z_o, east_o, west_o, south_o, north_o, msg):
+def middle(b, r, c, l, w, mflat, got, s2, s1, pre_o, z_o, east_o, west_o, south_o, north_o, wt, mwin, msg):
+    late_windows(w, mflat, got, s1, s2, wt, mwin)
     upper = lax.axis_index("core") == 0
     left, right = side_block(got, -1), side_block(got, 1)
     rows = 4 * HALO
@@ -245,7 +247,7 @@
     return jnp.where(row % 2 == 0, even, odd)
 
 
-def late_kernel(w, mflat, got, s1, s2, wt, mwin):
+def late_windows(w, mflat, got, s1, s2, wt, mwin):
     upper = lax.axis_index("core") == 0
     left, right = side_block(got, -1), side_block(got, 1)
     ww = halves(left, w, right, 4)
@@ -261,7 +263,7 @@
     for i, mine in enumerate((left[40:], mflat[...], right[40:])):
         at = slice(HALO * ncol + half * i, HALO * ncol + half * (i + 1))
         parts += [above[at], mine, below[at]]
-    mwin[...] = reordered(jnp.concatenate(parts, axis=0))
+    mwin[...] = jnp.concatenate(parts, axis=0)
 
 
 def last(xs, gathered, mwin, pre, z_i, wt, east, west, south, north, out):
@@ -338,11 +340,10 @@
     s2 = lax.ppermute(chip_msg, ROWAX, swap)
     s1 = lax.ppermute(core_msg, "core", [(0, 1), (1, 0)])
     win = f32(WROWS, wide)
-    pre, z, east, west, south, north, msg = call(middle, [win] * 6 + [f32(zs, 1, LANES)], 8, "middle")(
-        b, r, c, l, w, got, s2, s1
-    )
+    pre, z, east, west, south, north, wt, mwin, msg = call(
+        middle, [win] * 7 + [f32(24 * tiles, LANES), f32(zs, 1, LANES)], 9, "middle"
+    )(b, r, c, l, w, mflat, got, s2, s1)
     spread = lax.all_to_all(msg, "z", 0, 0, tiled=True)
-    wt, mwin = call(late_kernel, [win, f32(24 * tiles, LANES)], 5, "late")(w, mflat, got, s1, s2)
     line = jnp.sum(spread, axis=0)
     second = jnp.broadcast_to(line[None], (xs * cores * cols, 1, LANES))
     gathered = lax.all_to_all(second, ("x", "core", "cols"), 0, 0, tiled=True)

time: 88.3 us -> 87.8 us (level)
  blocking collectives: 50.4 us -> 65.7 us
  starting transfers between devices: 24.7 us -> 16.1 us
  waiting for transfers between devices: 7.4 us -> 1.06 us
    all_to_all x0 -> x1, blocking collectives: none -> 15.3 us  [local(): gathered = lax.all_to_all(second, ('x', 'core', 'cols'), 0, 0, tiled=True)]
    all_to_all x1 -> x0, starting transfers between devices: 8.56 us -> none  [local(): gathered = lax.all_to_all(second, ('x', 'core', 'cols'), 0, 0, tiled=True)]
    all_to_all x1 -> x0, waiting for transfers between devices: 6.34 us -> none  [local(): gathered = lax.all_to_all(second, ('x', 'core', 'cols'), 0, 0, tiled=True)]
  transfers between devices with their start and end apart: 3 -> 2, of which waited for: 2 -> 1; matrix products, arithmetic and copies ran while one was open for 0% -> 0% of each run, Pallas kernels for 1% -> 0%
where the time goes in v8:
time: 87.8 us; the launch traced here: 87.5 us
  blocking collectives  65.7 us (75%)
  starting transfers between devices  16.1 us (18%)
  Pallas kernels  4.41 us (5%)
  waiting for transfers between devices  1.06 us (1%)
    all_to_all x1, blocking collectives, local(): spread = lax.all_to_all(msg, 'z', 0, 0, tiled=True)  40.7 us
    all_to_all x1, blocking collectives, local(): gathered = lax.all_to_all(second, ('x', 'core', 'cols'), 0, 0, tiled=True)  15.3 us
    ppermute x1, starting transfers between devices, local(): s1 = lax.ppermute(core_msg, 'core', [(0, 1), (1, 0)])  10.6 us
    all_to_all x1, blocking collectives, local(): got = lax.all_to_all(edges, 'cols', 0, 0, tiled=True)  9.72 us
    ppermute x1, starting transfers between devices, local(): s2 = lax.ppermute(chip_msg, ROWAX, swap)  5.53 us
    pallas_call x1, Pallas kernels, local(): call(functools.partial(first_kernel, group), f32(cols, 8 + 4 * tiles, LAN...  2.04 us
  transfers between devices with their start and end apart: 2, of which 1 were waited for; matrix products, arithmetic and copies ran while one was open for 0% of the time, Pallas kernels for 0%

profile of v8, /device:TPU:1, one launch (start us, length us, event | category | flops | bytes accessed | tf_op | source)
XLA Modules:
  0.0 87.5 jit_solution(12824767828623142311)
XLA Ops:
  0.0 0.0 copy-start.2
  0.0 0.0 copy-start.3
  0.0 0.0 copy-start.4
  0.0 2.0 %first.1 = f32[4,40,128]{2,1,0:T(8,128)} custom-call(f32[8,2048]{1,0:T(8,128)} %b.3, f32[8,2048]{1,0:T(8,128)} %r.3, f32[8,2048]{1,0:T(8,128)} %c.3, f32[8,2048]{1,0:T(8,128)} %l.3, s32[192,128]{1,0:T(8,128)} %bitcast.2, f32[4,1024]{1,0:T(4,128)} %bitcast.4), custom_call_target="tpu_custom_call" | custom-call | tf_op jit(solution)/shard_map/first/pallas_call | solution.py:314
  2.1 0.0 copy-start
  2.1 0.0 copy-start.1
  2.1 0.0 copy-start.5
  2.1 9.7 %all_to_all.15.got = f32[4,40,128]{2,1,0:T(8,128)S(1)} all-to-all(f32[4,40,128]{2,1,0:T(8,128)} %first.1), channel_id=1, replica_groups=mesh['x'=4,'z'=32,'core'=2,'cols'=4] {'cols'}, dimensions={0} | all-to-all | bytes 163840 | tf_op jit(solution)/shard_map/all_to_all | solution.py:331
  11.8 0.0 copy-done.2
  11.8 0.0 copy-done.3
  11.8 0.0 copy-done.4
  11.8 0.0 copy-done
  11.8 0.0 copy-done.1
  11.8 0.0 copy-done.5
  11.9 0.4 rows.1
  12.3 5.5 %collective-permute-start = (f32[408,128]{1,0:T(8,128)S(1)}, f32[408,128]{1,0:T(8,128)S(1)}, u32[]{:S(2)}, u32[]{:S(2)}) collective-permute-start(f32[408,128]{1,0:T(8,128)S(1)} %get-tuple-element.20), channel_id=1, source_target_pairs={{4,8},{8,4},{12,16},{16,12},{20,24},{24,20},{28,32},{32,28},{36,40... | collective-permute-start | bytes 626696 | tf_op jit(solution)/shard_map/ppermute | solution.py:340
  17.8 10.6 %collective-permute-start.1 = (f32[408,128]{1,0:T(8,128)S(1)}, f32[408,128]{1,0:T(8,128)S(1)}, u32[]{:S(2)}, u32[]{:S(2)}) collective-permute-start(f32[408,128]{1,0:T(8,128)S(1)} %get-tuple-element.21), channel_id=1, source_target_pairs={{0,4},{4,0},{1,5},{5,1},{2,6},{6,2},{3,7},{7,3},{8,12},{12,8},{9,1... | collective-permute-start | bytes 626696 | tf_op jit(solution)/shard_map/ppermute | solution.py:341
  28.4 0.0 collective-permute-done.s2
  28.4 1.1 %collective-permute-done.1.s1 = f32[408,128]{1,0:T(8,128)S(1)} collective-permute-done((f32[408,128]{1,0:T(8,128)S(1)}, f32[408,128]{1,0:T(8,128)S(1)}, u32[]{:S(2)}, u32[]{:S(2)}) %collective-permute-start.1) | collective-permute-done | bytes 208928 | tf_op jit(solution)/shard_map/ppermute | solution.py:341
  29.5 0.8 middle.1
  30.2 40.7 %all_to_all.16 = f32[32,1,128]{2,1,0:T(1,128)S(1)} all-to-all(f32[32,1,128]{2,1,0:T(1,128)S(1)} %get-tuple-element.22), channel_id=1, replica_groups=mesh['x'=4,'z'=32,'core'=2,'cols'=4] {'z'}, dimensions={0} | all-to-all | bytes 32768 | tf_op jit(solution)/shard_map/all_to_all | solution.py:346
  70.9 0.1 reduce_sum.9
  71.0 15.3 %all_to_all.17.gathered = f32[32,1,128]{2,1,0:T(1,128)S(1)} all-to-all(f32[32,1,128]{2,1,0:T(1,128)S(1)} %broadcast_in_dim.2), channel_id=1, replica_groups=mesh['x'=4,'z'=32,'core'=2,'cols'=4] {'x','core','cols'}, dimensions={0} | all-to-all | bytes 32768 | tf_op jit(solution)/shard_map/all_to_all | solution.py:349
  86.3 1.2 %last.1 = f32[8,2048]{1,0:T(8,128)} custom-call(f32[32,1,128]{2,1,0:T(1,128)S(1)} %all_to_all.17.gathered, f32[192,128]{1,0:T(8,128)S(1)} %get-tuple-element.23.mwin, f32[16,2304]{1,0:T(8,128)S(1)} %get-tuple-element.24.pre, f32[16,2304]{1,0:T(8,128)S(1)} %get-tuple-element.25.z_i, f32[16,2304]{1,0:T(8,128)S(1)} %get-tuple-element.26.wt, ...), custom_call_target="tpu_custom_call" | custom-call | tf_op jit(solution)/shard_map/last/pallas_call | solution.py:350
  (1 shorter events, 0.0 us)
Async XLA Ops:
  0.0 11.8 %copy-start.2 = (f32[8,2048]{1,0:T(8,128)S(1)}, f32[8,2048]{1,0:T(8,128)}, u32[]{:S(2)}) copy-start(f32[8,2048]{1,0:T(8,128)} %c.3) | copy-start | bytes 196612
  0.0 11.8 %copy-start.3 = (f32[8,2048]{1,0:T(8,128)S(1)}, f32[8,2048]{1,0:T(8,128)}, u32[]{:S(2)}) copy-start(f32[8,2048]{1,0:T(8,128)} %l.3) | copy-start | bytes 196612
  0.0 11.8 %copy-start.4 = (s32[1,1,192,128]{3,2,1,0:T(8,128)S(1)}, s32[1,1,192,128]{3,2,1,0:T(8,128)}, u32[]{:S(2)}) copy-start(s32[1,1,192,128]{3,2,1,0:T(8,128)} %param.10) | copy-start | bytes 294916
  2.1 9.8 %copy-start = (f32[8,2048]{1,0:T(8,128)S(1)}, f32[8,2048]{1,0:T(8,128)}, u32[]{:S(2)}) copy-start(f32[8,2048]{1,0:T(8,128)} %b.3) | copy-start | bytes 196612
  2.1 9.8 %copy-start.1 = (f32[8,2048]{1,0:T(8,128)S(1)}, f32[8,2048]{1,0:T(8,128)}, u32[]{:S(2)}) copy-start(f32[8,2048]{1,0:T(8,128)} %r.3) | copy-start | bytes 196612
  2.1 9.8 %copy-start.5 = (f32[1,4,1024]{2,1,0:T(4,128)S(1)}, f32[1,4,1024]{2,1,0:T(4,128)}, u32[]{:S(2)}) copy-start(f32[1,4,1024]{2,1,0:T(4,128)} %param.11) | copy-start | bytes 49156
  12.3 16.1 %collective-permute-start = (f32[408,128]{1,0:T(8,128)S(1)}, f32[408,128]{1,0:T(8,128)S(1)}, u32[]{:S(2)}, u32[]{:S(2)}) collective-permute-start(f32[408,128]{1,0:T(8,128)S(1)} %get-tuple-element.20), channel_id=1, source_target_pairs={{4,8},{8,4},{12,16},{16,12},{20,24},{24,20},{28,32},{32,28},{36,40... | collective-permute-start | bytes 626696 | tf_op jit(solution)/shard_map/ppermute | solution.py:340
  17.8 11.7 %collective-permute-start.1 = (f32[408,128]{1,0:T(8,128)S(1)}, f32[408,128]{1,0:T(8,128)S(1)}, u32[]{:S(2)}, u32[]{:S(2)}) collective-permute-start(f32[408,128]{1,0:T(8,128)S(1)} %get-tuple-element.21), channel_id=1, source_target_pairs={{0,4},{4,0},{1,5},{5,1},{2,6},{6,2},{3,7},{7,3},{8,12},{12,8},{9,1... | collective-permute-start | bytes 626696 | tf_op jit(solution)/shard_map/ppermute | solution.py:341

commit v9 on v8

--- a/solution.py
+++ b/solution.py
@@ -143,9 +143,9 @@
     return up, down
 
 
-def rows_kernel(group, b, r, c, l, agg, m, got, chip_msg, core_msg, w, mflat):
+def rows_kernel(group, b, r, c, l, agg, got, chip_msg, core_msg, w, mflat):
     weights(group, agg, w)
-    flatten(m, mflat)
+    mflat[...] = got[lax.axis_index("cols")][8:]
     lower = lax.axis_index("core") == 1
     left, right = side_block(got, -1), side_block(got, 1)
     up, down = row_messages(b, r, c, l, left, right)
@@ -335,8 +335,8 @@
         swap += [(i, i + 1), (i + 1, i)]
     message = f32((4 * HALO + HALO) * wide // LANES + 6 * tiles, LANES)
     chip_msg, core_msg, w, mflat = call(
-        functools.partial(rows_kernel, group), [message, message, block, f32(4 * tiles, LANES)], 7, "rows"
-    )(b, r, c, l, agg, m, got)
+        functools.partial(rows_kernel, group), [message, message, block, f32(4 * tiles, LANES)], 6, "rows"
+    )(b, r, c, l, agg, got)
     s2 = lax.ppermute(chip_msg, ROWAX, swap)
     s1 = lax.ppermute(core_msg, "core", [(0, 1), (1, 0)])
     win = f32(WROWS, wide)

time: 87.8 us -> 87.7 us (level)
  no operation moved by 1% of the time
where the time goes in v9:
time: 87.7 us; the launch traced here: 87.3 us
  blocking collectives  65.7 us (75%)
  starting transfers between devices  16.1 us (18%)
  Pallas kernels  4.27 us (5%)
  waiting for transfers between devices  1.06 us (1%)
    all_to_all x1, blocking collectives, local(): spread = lax.all_to_all(msg, 'z', 0, 0, tiled=True)  40.7 us
    all_to_all x1, blocking collectives, local(): gathered = lax.all_to_all(second, ('x', 'core', 'cols'), 0, 0, tiled=True)  15.3 us
    ppermute x1, starting transfers between devices, local(): s1 = lax.ppermute(core_msg, 'core', [(0, 1), (1, 0)])  10.6 us
    all_to_all x1, blocking collectives, local(): got = lax.all_to_all(edges, 'cols', 0, 0, tiled=True)  9.72 us
    ppermute x1, starting transfers between devices, local(): s2 = lax.ppermute(chip_msg, ROWAX, swap)  5.54 us
    pallas_call x1, Pallas kernels, local(): call(functools.partial(first_kernel, group), f32(cols, 8 + 4 * tiles, LAN...  2.04 us
  transfers between devices with their start and end apart: 2, of which 1 were waited for; matrix products, arithmetic and copies ran while one was open for 0% of the time, Pallas kernels for 0%

profile of v9, /device:TPU:1, one launch (start us, length us, event | category | flops | bytes accessed | tf_op | source)
XLA Modules:
  0.0 87.3 jit_solution(10516972578382045386)
XLA Ops:
  0.0 0.0 copy-start.2
  0.0 0.0 copy-start.3
  0.0 0.0 copy-start.4
  0.0 2.0 %first.1 = f32[4,40,128]{2,1,0:T(8,128)} custom-call(f32[8,2048]{1,0:T(8,128)} %b.3, f32[8,2048]{1,0:T(8,128)} %r.3, f32[8,2048]{1,0:T(8,128)} %c.3, f32[8,2048]{1,0:T(8,128)} %l.3, s32[192,128]{1,0:T(8,128)} %bitcast.2, f32[4,1024]{1,0:T(4,128)} %bitcast.4), custom_call_target="tpu_custom_call" | custom-call | tf_op jit(solution)/shard_map/first/pallas_call | solution.py:314
  2.1 0.0 copy-start
  2.1 0.0 copy-start.1
  2.1 9.7 %all_to_all.15.got = f32[4,40,128]{2,1,0:T(8,128)S(1)} all-to-all(f32[4,40,128]{2,1,0:T(8,128)} %first.1), channel_id=1, replica_groups=mesh['x'=4,'z'=32,'core'=2,'cols'=4] {'cols'}, dimensions={0} | all-to-all | bytes 163840 | tf_op jit(solution)/shard_map/all_to_all | solution.py:331
  11.8 0.0 copy-done.2
  11.8 0.0 copy-done.3
  11.8 0.0 copy-done.4
  11.8 0.0 copy-done
  11.8 0.0 copy-done.1
  11.8 0.3 rows.1
  12.1 5.5 %collective-permute-start = (f32[408,128]{1,0:T(8,128)S(1)}, f32[408,128]{1,0:T(8,128)S(1)}, u32[]{:S(2)}, u32[]{:S(2)}) collective-permute-start(f32[408,128]{1,0:T(8,128)S(1)} %get-tuple-element.20), channel_id=1, source_target_pairs={{4,8},{8,4},{12,16},{16,12},{20,24},{24,20},{28,32},{32,28},{36,40... | collective-permute-start | bytes 626696 | tf_op jit(solution)/shard_map/ppermute | solution.py:340
  17.6 10.6 %collective-permute-start.1 = (f32[408,128]{1,0:T(8,128)S(1)}, f32[408,128]{1,0:T(8,128)S(1)}, u32[]{:S(2)}, u32[]{:S(2)}) collective-permute-start(f32[408,128]{1,0:T(8,128)S(1)} %get-tuple-element.21), channel_id=1, source_target_pairs={{0,4},{4,0},{1,5},{5,1},{2,6},{6,2},{3,7},{7,3},{8,12},{12,8},{9,1... | collective-permute-start | bytes 626696 | tf_op jit(solution)/shard_map/ppermute | solution.py:341
  28.3 0.0 collective-permute-done.s2
  28.3 1.1 %collective-permute-done.1.s1 = f32[408,128]{1,0:T(8,128)S(1)} collective-permute-done((f32[408,128]{1,0:T(8,128)S(1)}, f32[408,128]{1,0:T(8,128)S(1)}, u32[]{:S(2)}, u32[]{:S(2)}) %collective-permute-start.1) | collective-permute-done | bytes 208928 | tf_op jit(solution)/shard_map/ppermute | solution.py:341
  29.3 0.8 middle.1
  30.1 40.7 %all_to_all.16 = f32[32,1,128]{2,1,0:T(1,128)S(1)} all-to-all(f32[32,1,128]{2,1,0:T(1,128)S(1)} %get-tuple-element.22), channel_id=1, replica_groups=mesh['x'=4,'z'=32,'core'=2,'cols'=4] {'z'}, dimensions={0} | all-to-all | bytes 32768 | tf_op jit(solution)/shard_map/all_to_all | solution.py:346
  70.8 0.1 reduce_sum.9
  70.8 15.3 %all_to_all.17.gathered = f32[32,1,128]{2,1,0:T(1,128)S(1)} all-to-all(f32[32,1,128]{2,1,0:T(1,128)S(1)} %broadcast_in_dim.2), channel_id=1, replica_groups=mesh['x'=4,'z'=32,'core'=2,'cols'=4] {'x','core','cols'}, dimensions={0} | all-to-all | bytes 32768 | tf_op jit(solution)/shard_map/all_to_all | solution.py:349
  86.1 1.2 %last.1 = f32[8,2048]{1,0:T(8,128)} custom-call(f32[32,1,128]{2,1,0:T(1,128)S(1)} %all_to_all.17.gathered, f32[192,128]{1,0:T(8,128)S(1)} %get-tuple-element.23.mwin, f32[16,2304]{1,0:T(8,128)S(1)} %get-tuple-element.24.pre, f32[16,2304]{1,0:T(8,128)S(1)} %get-tuple-element.25.z_i, f32[16,2304]{1,0:T(8,128)S(1)} %get-tuple-element.26.wt, ...), custom_call_target="tpu_custom_call" | custom-call | tf_op jit(solution)/shard_map/last/pallas_call | solution.py:350
  (1 shorter events, 0.0 us)
Async XLA Ops:
  0.0 11.8 %copy-start.2 = (f32[8,2048]{1,0:T(8,128)S(1)}, f32[8,2048]{1,0:T(8,128)}, u32[]{:S(2)}) copy-start(f32[8,2048]{1,0:T(8,128)} %c.3) | copy-start | bytes 196612
  0.0 11.8 %copy-start.3 = (f32[8,2048]{1,0:T(8,128)S(1)}, f32[8,2048]{1,0:T(8,128)}, u32[]{:S(2)}) copy-start(f32[8,2048]{1,0:T(8,128)} %l.3) | copy-start | bytes 196612
  0.0 11.8 %copy-start.4 = (s32[1,1,192,128]{3,2,1,0:T(8,128)S(1)}, s32[1,1,192,128]{3,2,1,0:T(8,128)}, u32[]{:S(2)}) copy-start(s32[1,1,192,128]{3,2,1,0:T(8,128)} %param.10) | copy-start | bytes 294916
  2.1 9.8 %copy-start = (f32[8,2048]{1,0:T(8,128)S(1)}, f32[8,2048]{1,0:T(8,128)}, u32[]{:S(2)}) copy-start(f32[8,2048]{1,0:T(8,128)} %b.3) | copy-start | bytes 196612
  2.1 9.8 %copy-start.1 = (f32[8,2048]{1,0:T(8,128)S(1)}, f32[8,2048]{1,0:T(8,128)}, u32[]{:S(2)}) copy-start(f32[8,2048]{1,0:T(8,128)} %r.3) | copy-start | bytes 196612
  12.1 16.2 %collective-permute-start = (f32[408,128]{1,0:T(8,128)S(1)}, f32[408,128]{1,0:T(8,128)S(1)}, u32[]{:S(2)}, u32[]{:S(2)}) collective-permute-start(f32[408,128]{1,0:T(8,128)S(1)} %get-tuple-element.20), channel_id=1, source_target_pairs={{4,8},{8,4},{12,16},{16,12},{20,24},{24,20},{28,32},{32,28},{36,40... | collective-permute-start | bytes 626696 | tf_op jit(solution)/shard_map/ppermute | solution.py:340
  17.6 11.7 %collective-permute-start.1 = (f32[408,128]{1,0:T(8,128)S(1)}, f32[408,128]{1,0:T(8,128)S(1)}, u32[]{:S(2)}, u32[]{:S(2)}) collective-permute-start(f32[408,128]{1,0:T(8,128)S(1)} %get-tuple-element.21), channel_id=1, source_target_pairs={{0,4},{4,0},{1,5},{5,1},{2,6},{6,2},{3,7},{7,3},{8,12},{12,8},{9,1... | collective-permute-start | bytes 626696 | tf_op jit(solution)/shard_map/ppermute | solution.py:341
